TPU v7x, 32 devices: a whole 2x2x4 slice. The times are simulated.
32 devices in a mesh: node: 8 (over y, x, core), batch: 4 (over z).
Axes of the slice: x: 2, y: 2, z: 4, core: 2. Of those that a mesh axis runs over, the one named last changes fastest.
Arguments:
- memory: bfloat16 [65536, 128], P('node'), may hold values from -5 to 5
- src_owner: int32 [16384, 1], P(('node', 'batch')), may hold values from 0 to 7; in each aligned block of 512 rows (0 to 511, 512 to 1023, ...) at most 128 rows name the same one
- src_row: int32 [16384], P(('node', 'batch')), may hold values from 0 to 8191
- fetch_owner: int32 [16384, 11, 1], P(('node', 'batch')), may hold values from 0 to 7; in each aligned block of 5632 rows (0 to 5631, 5632 to 11263, ..., all dimensions but the last counted through in order) at most 1408 rows name the same one
- fetch_row: int32 [16384, 11], P(('node', 'batch')), may hold values from 0 to 8191
- event_tick: int32 [16384], P(('node', 'batch')), may hold values from 5000 to 9999
- source_tick: int32 [16384], P(('node', 'batch')), may hold values from 0 to 4999
- neighbour_tick: int32 [16384, 10], P(('node', 'batch')), may hold values from 0 to 4999
- time_freq: float32 [128], replicated, may hold values from 0.0001 to 0.1
- time_phase: float32 [128], replicated, may hold values from -3.140625 to 3.140625
- gru_input: bfloat16 [256, 384], replicated, may hold values from -0.375 to 0.375
- gru_hidden: bfloat16 [128, 384], replicated, may hold values from -0.5 to 0.5
- gru_bias: float32 [512], replicated, may hold values from -3 to 3
- w_query: bfloat16 [128, 128], replicated, may hold values from -0.5 to 0.5
- w_kv: bfloat16 [256, 256], replicated, may hold values from -0.375 to 0.375
- w_merge: bfloat16 [256, 128], replicated, may hold values from -0.375 to 0.375
- merge_bias: float32 [128], replicated, may hold values from -3 to 3
- out_grad: float32 [16384, 128], P(('node', 'batch')), may hold values from -0.02 to 0.02
Outputs:
- embedding: float32 [16384, 128], P(('node', 'batch'))
- memory_out: bfloat16 [65536, 128], P('node')
- grad_query: float32 [128, 128], replicated
- grad_kv: float32 [256, 256], replicated
- grad_merge: float32 [256, 128], replicated
- grad_bias: float32 [128], replicated
Inputs may be any that keep to these rules, and one draw needn't show every extreme that they name: `src_owner`: among the 512 events of one device no owner is named by more than 128 of them. `fetch_owner`: among the 512 * (11) entries of one device no owner is named by more than 1408 of them.
All inputs are finite; a program needn't handle non-finite values.
Results may differ from a plain program's by a relative error of at most 0.012.
Values may be sent and summed in bfloat16 or wider, within the bound.
A program may use at most 64 MiB of HBM per device.

v0:
```python
import math

import jax
import jax.numpy as jnp
from jax import lax
from jax.sharding import PartitionSpec as P

HEADS = 2


def time_code(delta, freq, phase):
    return jnp.cos(delta[..., None] * freq + phase)


def gru_cell(message, state, gru_input, gru_hidden, gru_bias):
    width = state.shape[-1]
    from_msg = (
        jnp.dot(message, gru_input, preferred_element_type=jnp.float32) + gru_bias[: 3 * width]
    )
    from_state = jnp.dot(state, gru_hidden, preferred_element_type=jnp.float32)
    reset = jax.nn.sigmoid(from_msg[:, :width] + from_state[:, :width])
    update = jax.nn.sigmoid(from_msg[:, width : 2 * width] + from_state[:, width : 2 * width])
    candid = jnp.tanh(
        from_msg[:, 2 * width :] + reset * (from_state[:, 2 * width :] + gru_bias[3 * width :])
    )
    return ((1.0 - update) * candid + update * state.astype(jnp.float32)).astype(jnp.bfloat16)


def last_pick(owner_ids, row_ids):
    same = (owner_ids[:, None] == owner_ids[None, :]) & (row_ids[:, None] == row_ids[None, :])
    places = jnp.arange(owner_ids.shape[0], dtype=jnp.int32)
    return jnp.max(jnp.where(same, places[None, :], jnp.int32(-1)), axis=1)


def place(owner_ids, owner_count, capacity):
    onehot = (owner_ids[:, None] == jnp.arange(owner_count, dtype=jnp.int32)[None, :]).astype(
        jnp.int32
    )
    before = jnp.cumsum(onehot, axis=0) - onehot
    return owner_ids * capacity + jnp.sum(before * onehot, axis=1)


def embed(query_w, pair_w, merge_w, bias_term, new_src, kv_in):
    att_width = query_w.shape[1]
    head_width = att_width // HEADS
    row_count = new_src.shape[0]
    nb_count = kv_in.shape[1]
    query_rows = jnp.dot(new_src, query_w.astype(jnp.bfloat16), preferred_element_type=jnp.float32)
    pairs = jnp.dot(kv_in, pair_w.astype(jnp.bfloat16), preferred_element_type=jnp.float32)
    key_rows = pairs[..., :att_width].reshape(row_count, nb_count, HEADS, head_width)
    value_rows = pairs[..., att_width:].reshape(row_count, nb_count, HEADS, head_width)
    scores = jnp.einsum(
        "ehd,enhd->ehn", query_rows.reshape(row_count, HEADS, head_width), key_rows
    ) / math.sqrt(head_width)
    scores = scores - jnp.max(scores, axis=-1, keepdims=True)
    shares = jnp.exp(scores)
    shares = shares / jnp.sum(shares, axis=-1, keepdims=True)
    mixed = (
        jnp.einsum("ehn,enhd->ehd", shares, value_rows)
        .reshape(row_count, att_width)
        .astype(jnp.bfloat16)
    )
    joined = jnp.concatenate([mixed, new_src], axis=-1)
    return jax.nn.silu(
        jnp.dot(joined, merge_w.astype(jnp.bfloat16), preferred_element_type=jnp.float32)
        + bias_term
    )


def on_device(
    memory,
    src_owner,
    src_row,
    fetch_owner,
    fetch_row,
    event_tick,
    source_tick,
    neighbour_tick,
    time_freq,
    time_phase,
    gru_input,
    gru_hidden,
    gru_bias,
    w_query,
    w_kv,
    w_merge,
    merge_bias,
    out_grad,
):
    owner_count = lax.axis_size("node")
    batch_count = lax.axis_size("batch")
    batch_place = lax.axis_index("batch")
    event_count = src_row.shape[0]
    per_event = fetch_row.shape[1]
    mem_width = memory.shape[1]
    node_local = memory.shape[0]
    far_cap = event_count * per_event * 2 // owner_count
    near_cap = event_count * 2 // owner_count
    near_owner = src_owner[:, 0]
    far_slot = place(fetch_owner.reshape(-1), owner_count, far_cap)
    near_slot = place(near_owner, owner_count, near_cap)
    far_ask = (
        jnp.zeros((owner_count * far_cap,), jnp.int32)
        .at[far_slot]
        .set(fetch_row.reshape(-1))
        .reshape(owner_count, far_cap)
    )
    near_ask = (
        jnp.zeros((owner_count * near_cap,), jnp.int32)
        .at[near_slot]
        .set(src_row + 1)
        .reshape(owner_count, near_cap)
    )
    far_got, near_got = (
        lax.all_to_all(far_ask, "node", split_axis=0, concat_axis=0, tiled=True),
        lax.all_to_all(near_ask, "node", split_axis=0, concat_axis=0, tiled=True),
    )
    near_flat = near_got.reshape(-1)
    near_live = near_flat > 0
    near_index = jnp.maximum(near_flat - 1, 0)
    far_rows = memory[far_got]
    near_rows = memory[near_index].reshape(owner_count, near_cap, mem_width)
    source_code = time_code(
        (event_tick - source_tick).astype(jnp.float32), time_freq, time_phase
    ).astype(jnp.bfloat16)
    far_back = lax.all_to_all(far_rows, "node", split_axis=0, concat_axis=0, tiled=True)
    fetched = far_back.reshape(owner_count * far_cap, mem_width)[far_slot].reshape(
        event_count, per_event, mem_width
    )
    message = jnp.concatenate([fetched[:, 0], source_code], axis=-1)
    msg_width = message.shape[1]
    outgoing = (
        jnp.zeros((owner_count * near_cap, msg_width), jnp.bfloat16)
        .at[near_slot]
        .set(message)
        .reshape(owner_count, near_cap, msg_width)
    )
    arrived = lax.all_to_all(outgoing, "node", split_axis=0, concat_axis=0, tiled=True)
    fresh = gru_cell(
        arrived.reshape(-1, msg_width),
        near_rows.reshape(-1, mem_width),
        gru_input,
        gru_hidden,
        gru_bias,
    )
    returned = lax.all_to_all(
        fresh.reshape(owner_count, near_cap, mem_width),
        "node",
        split_axis=0,
        concat_axis=0,
        tiled=True,
    )
    updated = returned.reshape(owner_count * near_cap, mem_width)[near_slot]
    sender_ids = jnp.repeat(jnp.arange(owner_count, dtype=jnp.int32), near_cap)
    slot_ids = jnp.tile(jnp.arange(near_cap, dtype=jnp.int32), owner_count)
    priority = (sender_ids * batch_count + batch_place) * near_cap + slot_ids
    packed = jnp.where(near_live, priority * node_local + near_index, jnp.int32(-1))
    all_fresh, all_keys = (
        lax.all_gather(fresh, "batch", axis=0, tiled=True),
        lax.all_gather(packed, "batch", axis=0, tiled=True),
    )
    key_live = all_keys >= 0
    key_rows = jnp.where(key_live, all_keys % node_local, node_local).astype(jnp.int32)
    best = jnp.full((node_local + 1,), -1, jnp.int32).at[key_rows].max(all_keys)
    winner = key_live & (all_keys == best[key_rows])
    target = jnp.where(winner, key_rows, node_local)
    memory_out = memory.at[target].set(all_fresh, mode="drop")
    new_src = updated[last_pick(near_owner, src_row)]
    nb_code = time_code(
        (event_tick[:, None] - neighbour_tick).astype(jnp.float32), time_freq, time_phase
    ).astype(jnp.bfloat16)
    kv_in = jnp.concatenate([fetched[:, 1:], nb_code], axis=-1)

    def forward(query_w, pair_w, merge_w, bias_term):
        return embed(query_w, pair_w, merge_w, bias_term, new_src, kv_in)

    result, pull = jax.vjp(
        forward,
        w_query.astype(jnp.float32),
        w_kv.astype(jnp.float32),
        w_merge.astype(jnp.float32),
        merge_bias,
    )
    grads = pull(out_grad)
    summed = lax.psum((grads[0], grads[1], grads[2], grads[3]), ("node", "batch"))
    return (result, memory_out, summed[0], summed[1], summed[2], summed[3])


def solution(mesh):
    return jax.shard_map(
        on_device,
        mesh=mesh,
        in_specs=(
            P("node", None),
            P(("node", "batch"), None),
            P(("node", "batch")),
            P(("node", "batch"), None, None),
            P(("node", "batch"), None),
            P(("node", "batch")),
            P(("node", "batch")),
            P(("node", "batch"), None),
            P(),
            P(),
            P(),
            P(),
            P(),
            P(),
            P(),
            P(),
            P(),
            P(("node", "batch"), None),
        ),
        out_specs=(P(("node", "batch"), None), P("node", None), P(), P(), P(), P()),
        check_vma=False,
    )
```

profile of v0, /device:TPU:0, one launch (start us, length us, event | category | flops | bytes accessed | tf_op | source)
XLA Modules:
  0.0 347.9 jit_solution(14605585450725997113)
XLA Ops:
  8.0 1.6 copy.109
  10.7 2.4 reduce-window.16
  14.3 21.1 %scatter_custom_fusion = s32[11264]{0:T(1024)S(1)} fusion(s32[5632]{0:T(1024)S(1)} %fusion.43, s32[5632]{0:T(1024)S(1)} %reshape.304, s32[]{:T(128)} %constant.24.clone.1), kind=kCustom, calls=%fused_computation.91 | custom fusion | bytes 45060 | tf_op jit(solution)/shard_map/scatter | solution.py:105
  35.4 9.9 %all_to_all.36 = s32[8,1,1408]{2,1,0:T(1,128)S(1)} all-to-all(s32[8,1,1408]{2,1,0:T(1,128)S(1)} %bitcast.125), channel_id=1, replica_groups=mesh['node'=8,'batch'=4] {'node'}, dimensions={0} | all-to-all | bytes 90112 | tf_op jit(solution)/shard_map/all_to_all | solution.py:115
  45.4 39.8 %gather_fusion = bf16[11264,128]{1,0:T(8,128)(2,1)} fusion(bf16[8192,128]{1,0:T(8,128)(2,1)S(1)} %copy.109, s32[11264]{0:T(1024)S(1)} %broadcast_clamp_fusion), kind=kCustom, calls=%fused_computation | custom fusion | bytes 5812224 | tf_op jit(solution)/shard_map/gather | solution.py:121
  85.2 4.6 %all-to-all-start.1 = ((bf16[8,1408,128]{2,1,0:T(8,128)(2,1)}), bf16[8,1408,128]{2,1,0:T(8,128)(2,1)}, u32[]{:S(2)}, u32[]{:S(2)}) async-start(bf16[8,1408,128]{2,1,0:T(8,128)(2,1)} %bitcast.114), calls=%async_computation.1 | async-start | bytes 5767168 | tf_op jit(solution)/shard_map/all_to_all | solution.py:126
  89.8 1.1 reduce-window.14
  91.4 3.0 scatter_custom_fusion.2
  94.4 0.4 select_reduce_fusion
  94.9 0.9 cosine_convert_fusion.1
  95.8 10.1 %cosine_convert_fusion = bf16[512,10,128]{2,0,1:T(8,128)(2,1)} fusion(f32[128]{0:T(128)S(1)} %copy-done.17, f32[128]{0:T(128)S(1)} %copy-done.18, f32[512,10]{0,1:T(8,128)S(1)} %subtract_convert_fusion), kind=kLoop, calls=%fused_computation.20 | loop fusion | flops 1966080 | bytes 1332224 | tf_op jit(solution)/shard_map/convert_element_type | solution.py:171
  105.9 19.0 %all-to-all-done.1 = bf16[8,1408,128]{2,1,0:T(8,128)(2,1)} async-done(((bf16[8,1408,128]{2,1,0:T(8,128)(2,1)}), bf16[8,1408,128]{2,1,0:T(8,128)(2,1)}, u32[]{:S(2)}, u32[]{:S(2)}) %all-to-all-start.1) | async-done | bytes 2883616 | tf_op jit(solution)/shard_map/all_to_all | solution.py:126
  124.9 3.3 all-to-all-start.3
  128.3 13.4 %gather_fusion.1 = bf16[5632,128]{1,0:T(8,128)(2,1)} fusion(bf16[11264,128]{1,0:T(8,128)(2,1)} %bitcast.15, s32[6144]{0:T(1024)S(1)} %pad_clamp_fusion), kind=kCustom, calls=%fused_computation.1 | custom fusion | bytes 2906112 | tf_op jit(solution)/shard_map/gather | solution.py:127
  141.6 3.7 %reshape.238 = bf16[512,11,128]{2,1,0:T(8,128)(2,1)} reshape(bf16[5632,128]{1,0:T(8,128)(2,1)} %gather_fusion.1) | data formatting | bytes 2883584 | tf_op jit(solution)/shard_map/reshape | solution.py:127
  145.3 1.4 slice.78
  146.7 3.2 scatter_custom_fusion.1
  149.9 4.1 %all-to-all-start.2 = ((bf16[8,128,256]{2,1,0:T(8,128)(2,1)}), bf16[8,128,256]{2,1,0:T(8,128)(2,1)S(1)}, u32[]{:S(2)}, u32[]{:S(2)}) async-start(bf16[8,128,256]{2,1,0:T(8,128)(2,1)} %bitcast.16), calls=%async_computation.2 | async-start | bytes 1048576 | tf_op jit(solution)/shard_map/all_to_all | solution.py:138
  154.0 3.2 gather_fusion.2
  157.3 13.5 %all_gather.6 = s32[4096]{0:T(1024)S(1)} all-gather(s32[1024]{0:T(1024)S(1)} %get-tuple-element.24), channel_id=1, replica_groups=mesh['node'=8,'batch'=4] {'batch'}, dimensions={0}, use_global_device_ids=true | all-gather | bytes 20480 | tf_op jit(solution)/shard_map/all_gather | solution.py:160
  170.8 1.5 fusion.65
  172.3 2.6 slice.85
  174.9 1.4 copy.95
  176.3 0.4 convolution_add_fusion
  176.7 1.0 copy-done.4
  177.7 1.1 fusion.21
  178.8 4.2 %all-to-all-start.4 = ((bf16[8,128,128]{2,1,0:T(8,128)(2,1)}), bf16[8,128,128]{2,1,0:T(8,128)(2,1)S(1)}, u32[]{:S(2)}, u32[]{:S(2)}) async-start(bf16[8,128,128]{2,1,0:T(8,128)(2,1)} %bitcast.21), calls=%async_computation.4 | async-start | bytes 524288 | tf_op jit(solution)/shard_map/all_to_all | solution.py:146
  183.0 2.6 fusion.4
  185.6 2.3 copy-done.2
  188.0 1.9 all-to-all-done.4
  189.9 1.3 gather_fusion.3
  191.2 1.3 gather_fusion.4
  192.8 4.0 %multiply_reduce_fusion.3 = (f32[512,2,10]{0,1,2:T(2,128)S(1)}, f32[512,10,128]{0,2,1:T(8,128)}) fusion(f32[512,2,64]{0,2,1:T(8,128)S(1)} %bitcast.119, f32[512,10,256]{0,2,1:T(8,128)} %copy-done.2), kind=kLoop, calls=%fused_computation.19 | loop fusion | flops 1300480 | bytes 5545984 | tf_op jit(solution)/shard_map/jvp(ehd,enhd->ehn)/dot_general | solution.py:52
  197.8 1.0 fusion.62
  199.1 2.6 broadcast_multiply_fusion.1
  201.9 0.9 fusion.14
  202.8 0.4 broadcast_multiply_fusion
  203.3 0.9 fusion.15
  204.2 0.4 copy-done.6
  204.6 1.6 fusion.11
  206.2 23.5 %scatter_custom_fusion.3 = s32[8193]{0:T(1024)S(1)} fusion(s32[4096]{0:T(1024)S(1)} %get-tuple-element.23, s32[4096]{0:T(1024)S(1)} %all_gather.6, s32[]{:T(128)} %constant.30.clone.1), kind=kCustom, calls=%fused_computation.96 | custom fusion | flops 4096 | bytes 32776 | tf_op jit(solution)/shard_map/scatter-max | solution.py:164
  229.7 23.0 %gather_fusion.5 = s32[4096]{0:T(1024)S(1)} fusion(s32[8193]{0:T(1024)S(1)} %scatter_custom_fusion.3, s32[4096]{0:T(1024)S(1)} %get-tuple-element.22), kind=kCustom, calls=%fused_computation.5 | custom fusion | bytes 49152 | tf_op jit(solution)/shard_map/gather | solution.py:165
  252.7 41.7 %psum.31 = f32[128]{0:T(128)} all-reduce(f32[128]{0:T(128)S(1)} %get-tuple-element.11), channel_id=1, replica_groups=mesh['node'=8,'batch'=4] {'node','batch'}, use_global_device_ids=true, to_apply=%region_21.22 | all-reduce | flops 128 | bytes 1024 | tf_op jit(solution)/shard_map/psum | solution.py:185
  294.4 12.5 %scatter_fusion = bf16[8192,128]{1,0:T(8,128)(2,1)S(1)} fusion(bf16[8192,128]{1,0:T(8,128)(2,1)S(1)} %copy.109, s32[4096]{0:T(1024)S(1)} %compare_select_fusion.2, bf16[4096,128]{1,0:T(8,128)(2,1)} %all-gather.2.cloned.1.call-done), kind=kCustom, calls=%fused_computation.10 | custom fusion | bytes 3162112 | tf_op jit(solution)/shard_map/scatter | solution.py:167
  306.9 28.8 %all-reduce.5.cloned.1.call-done = (f32[128,128]{1,0:T(8,128)}, f32[256,256]{1,0:T(8,128)}, f32[256,128]{1,0:T(8,128)}) async-done(((f32[128,128]{1,0:T(8,128)}, f32[256,256]{1,0:T(8,128)}, f32[256,128]{1,0:T(8,128)}), (f32[128,128]{1,0:T(8,128)}, f32[256,256]{1,0:T(8,128)}, f32[256,128]{1,0:T(8,128)})) %all-reduce.5.cloned.1.call-update) | async-done | bytes 458768 | tf_op jit(solution)/shard_map/psum | solution.py:185
  335.7 1.5 copy.110
  337.2 1.7 copy.111
  338.8 1.6 copy.112
  (100 shorter events, 4.5 us)
Async XLA Ops:
  8.0 168.3 %copy-start = (bf16[256,384]{1,0:T(8,128)(2,1)S(1)}, bf16[256,384]{1,0:T(8,128)(2,1)}, u32[]{:S(2)}) copy-start(bf16[256,384]{1,0:T(8,128)(2,1)} %param.28) | copy-start | bytes 589828
  8.0 1.7 copy-start.9
  8.0 5.7 %copy-start.12 = (s32[512,11]{0,1:T(8,128)S(1)}, s32[512,11]{0,1:T(8,128)}, u32[]{:S(2)}) copy-start(s32[512,11]{0,1:T(8,128)} %param.22) | copy-start | bytes 67588
  85.2 4.6 %copy-start.11 = (s32[512,1]{0,1:T(1,128)S(1)}, s32[512,1]{0,1:T(1,128)}, u32[]{:S(2)}) copy-start(s32[512,1]{0,1:T(1,128)} %param.19) | copy-start | bytes 6148
  85.2 6.1 %copy-start.15 = (s32[512]{0:T(512)S(1)}, s32[512]{0:T(512)}, u32[]{:S(2)}) copy-start(s32[512]{0:T(512)} %param.20) | copy-start | bytes 6148
  85.2 9.6 %copy-start.16 = (s32[512]{0:T(512)S(1)}, s32[512]{0:T(512)}, u32[]{:S(2)}) copy-start(s32[512]{0:T(512)} %param.23) | copy-start | bytes 6148
  85.2 9.6 %copy-start.19 = (s32[512]{0:T(512)S(1)}, s32[512]{0:T(512)}, u32[]{:S(2)}) copy-start(s32[512]{0:T(512)} %param.24) | copy-start | bytes 6148
  85.2 9.6 %copy-start.13 = (s32[512,10]{0,1:T(8,128)S(1)}, s32[512,10]{0,1:T(8,128)}, u32[]{:S(2)}) copy-start(s32[512,10]{0,1:T(8,128)} %param.25) | copy-start | bytes 61444
  85.2 9.6 %copy-start.17 = (f32[128]{0:T(128)S(1)}, f32[128]{0:T(128)}, u32[]{:S(2)}) copy-start(f32[128]{0:T(128)} %param.27) | copy-start | bytes 1540
  85.2 9.6 %copy-start.18 = (f32[128]{0:T(128)S(1)}, f32[128]{0:T(128)}, u32[]{:S(2)}) copy-start(f32[128]{0:T(128)} %param.26) | copy-start | bytes 1540
  85.2 43.0 %copy-start.20 = (f32[512]{0:T(512)S(1)}, f32[512]{0:T(512)}, u32[]{:S(2)}) copy-start(f32[512]{0:T(512)} %param.30) | copy-start | bytes 6148
  85.2 39.6 %all-to-all-start.1 = ((bf16[8,1408,128]{2,1,0:T(8,128)(2,1)}), bf16[8,1408,128]{2,1,0:T(8,128)(2,1)}, u32[]{:S(2)}, u32[]{:S(2)}) async-start(bf16[8,1408,128]{2,1,0:T(8,128)(2,1)} %bitcast.114), calls=%async_computation.1 | async-start | bytes 5767168 | tf_op jit(solution)/shard_map/all_to_all | solution.py:126
  124.9 25.0 %all-to-all-start.3 = ((s32[8,1,128]{2,1,0:T(1,128)}), s32[8,1,128]{2,1,0:T(1,128)S(1)}, u32[]{:S(2)}, u32[]{:S(2)}) async-start(s32[8,1,128]{2,1,0:T(1,128)} %bitcast.18), calls=%async_computation.3 | async-start | bytes 8192 | tf_op jit(solution)/shard_map/all_to_all | solution.py:116
  145.3 25.5 %copy-start.8 = (bf16[128,384]{1,0:T(8,128)(2,1)S(1)}, bf16[128,384]{1,0:T(8,128)(2,1)}, u32[]{:S(2)}) copy-start(bf16[128,384]{1,0:T(8,128)(2,1)} %param.29) | copy-start | bytes 294916
  149.9 26.4 %all-to-all-start.2 = ((bf16[8,128,256]{2,1,0:T(8,128)(2,1)}), bf16[8,128,256]{2,1,0:T(8,128)(2,1)S(1)}, u32[]{:S(2)}, u32[]{:S(2)}) async-start(bf16[8,128,256]{2,1,0:T(8,128)(2,1)} %bitcast.16), calls=%async_computation.2 | async-start | bytes 1048576 | tf_op jit(solution)/shard_map/all_to_all | solution.py:138
  176.3 1.4 copy-start.4
  177.7 5.3 %copy-start.7 = (bf16[256,256]{1,0:T(8,128)(2,1)S(1)}, bf16[256,256]{1,0:T(8,128)(2,1)}, u32[]{:S(2)}) copy-start(bf16[256,256]{1,0:T(8,128)(2,1)} %param.32) | copy-start | bytes 393220
  178.8 11.1 %all-to-all-start.4 = ((bf16[8,128,128]{2,1,0:T(8,128)(2,1)}), bf16[8,128,128]{2,1,0:T(8,128)(2,1)S(1)}, u32[]{:S(2)}, u32[]{:S(2)}) async-start(bf16[8,128,128]{2,1,0:T(8,128)(2,1)} %bitcast.21), calls=%async_computation.4 | async-start | bytes 524288 | tf_op jit(solution)/shard_map/all_to_all | solution.py:146
  182.9 111.5 %all-gather.2.cloned.1.call-start = ((), (), s32[]{:S(2)}) async-start(), calls=%async_computation.5 | async-start | bytes 1310720 | tf_op jit(solution)/shard_map/all_gather | solution.py:159
  185.6 2.3 copy-start.2
  187.9 4.7 %copy-start.14 = (bf16[128,128]{1,0:T(8,128)(2,1)S(1)}, bf16[128,128]{1,0:T(8,128)(2,1)}, u32[]{:S(2)}) copy-start(bf16[128,128]{1,0:T(8,128)(2,1)} %param.31) | copy-start | bytes 98308
  187.9 147.8 %all-reduce.5.cloned.1.call-start = ((), (), s32[]{:S(2)}) async-start(), calls=%async_computation.6 | async-start | bytes 917504 | tf_op jit(solution)/shard_map/psum | solution.py:185
  192.8 4.2 %slice-start = ((f32[512,10,256]{0,2,1:T(8,128)}), f32[512,10,128]{0,2,1:T(8,128)S(1)}, s32[]{:S(2)}) async-start(f32[512,10,256]{0,2,1:T(8,128)} %copy-done.2), calls=%async_computation.7 | async-start | bytes 5242880 | tf_op jit(solution)/shard_map/jvp()/slice | solution.py:51
  196.8 0.8 copy-start.10
  196.8 1.0 copy-start.21
  196.9 1.0 copy-start.22
  199.1 3.7 %copy-start.3 = (f32[512,10,128]{0,2,1:T(8,128)S(1)}, f32[512,10,128]{0,2,1:T(8,128)}, u32[]{:S(2)}) copy-start(f32[512,10,128]{0,2,1:T(8,128)} %get-tuple-element.16) | copy-start | bytes 7864324
  202.8 1.3 copy-start.5
  202.8 1.8 copy-start.6
  306.9 33.5 %copy-start.1 = (bf16[8192,128]{1,0:T(8,128)(2,1)}, bf16[8192,128]{1,0:T(8,128)(2,1)S(1)}, u32[]{:S(2)}) copy-start(bf16[8192,128]{1,0:T(8,128)(2,1)S(1)} %scatter_fusion) | copy-start | bytes 6291460
Sparse Core Ops, SparseCore 0:
  188.1 30.3 all-gather.1
Sparse Core Ops, SparseCore 1:
  206.3 129.4 all-reduce.4
where the time goes:
time: 349 us; the launch traced here: 348 us
  local copies, waits for them, and re-layouts  140 us (40%)
  blocking collectives  65.1 us (19%)
  other arithmetic  51.1 us (15%)
  waiting for transfers between devices  49.7 us (14%)
  starting transfers between devices  16.3 us (5%)
  between operations  16.1 us (5%)
  matrix products  9.36 us (3%)
    psum x1, blocking collectives, on_device(): lax.psum((grads[0], grads[1], grads[2], grads[3]), ('node', 'batch'))  41.7 us
    gather x1, local copies, waits for them, and re-layouts, on_device(): far_rows = memory[far_got]  39.8 us
    psum x1, waiting for transfers between devices, on_device(): lax.psum((grads[0], grads[1], grads[2], grads[3]), ('node', 'batch'))  28.8 us
    another operation x1, other arithmetic, on_device(): best = jnp.full((node_local + 1,), -1, jnp.int32).at[key_rows].max(all_keys)  23.5 us
    gather x1, local copies, waits for them, and re-layouts, on_device(): winner = key_live & (all_keys == best[key_rows])  23 us
    scatter x1, local copies, waits for them, and re-layouts, on_device(): far_ask = jnp.zeros((owner_count * far_cap,), jnp.int32).at[far_slot].set...  21.1 us
    all_to_all x1, waiting for transfers between devices, on_device(): lax.all_to_all(far_rows, 'node', split_axis=0, concat_axis=0, tiled=True)  19 us
    all_gather x1, blocking collectives, on_device(): lax.all_gather(packed, 'batch', axis=0, tiled=True)  13.5 us
  transfers between devices with their start and end apart: 6, of which 3 were waited for; matrix products, arithmetic and copies ran while one was open for 35% of the time, Pallas kernels for 0%

commit v1 on v0

v1 whole, which is shorter than its diff:
```python
import functools
import math

import jax
import jax.numpy as jnp
from jax import lax
from jax.experimental import pallas as pl
from jax.experimental.pallas import tpu as pltpu
from jax.sharding import PartitionSpec as P

HEADS = 2
LANES = 128
F32 = jnp.float32
BF16 = jnp.bfloat16
VMEM = pltpu.VMEM
SMEM = pltpu.SMEM
COS_TERMS = [(-1.0) ** k * (2 * math.pi) ** (2 * k) / math.factorial(2 * k) for k in range(9)]


def cos_code(delta, freq, phase):
    turns = delta[..., None] * (freq * (0.5 / math.pi)) + phase * (0.5 / math.pi)
    turns = turns - jnp.round(turns)
    square = turns * turns
    total = jnp.full_like(square, COS_TERMS[-1])
    for term in COS_TERMS[-2::-1]:
        total = total * square + term
    return total.astype(BF16)


def ranks(owner_grid, owner_count):
    rows, lanes = owner_grid.shape
    masks = (owner_grid[None] == jnp.arange(owner_count, dtype=jnp.int32)[:, None, None]).astype(BF16)
    lane_before = jnp.triu(jnp.ones((lanes, lanes), BF16), 1)
    row_before = jnp.triu(jnp.ones((rows, rows), BF16), 1)
    within = jnp.einsum("orl,lm->orm", masks, lane_before, preferred_element_type=F32)
    totals = jnp.sum(masks.astype(F32), axis=-1).astype(BF16)
    base = jnp.einsum("or,rs->os", totals, row_before, preferred_element_type=F32)
    return jnp.sum(masks.astype(F32) * (within + base[:, :, None]), axis=0).astype(jnp.int32)


def spread(slot, value, slot_count):
    hi, lo = slot // LANES, slot % LANES
    bump = value + 1
    at_hi = hi[None, :] == jnp.arange(slot_count // LANES, dtype=jnp.int32)[:, None]
    upper = jnp.where(at_hi, (bump // 64).astype(F32)[None, :], 0.0).astype(BF16)
    lower = jnp.where(at_hi, (bump % 64).astype(F32)[None, :], 0.0).astype(BF16)
    at_lo = (lo[None, :] == jnp.arange(LANES, dtype=jnp.int32)[:, None]).astype(BF16)
    both = jnp.einsum(
        "he,le->hl", jnp.concatenate([upper, lower], 0), at_lo, preferred_element_type=F32
    ).astype(jnp.int32)
    half = slot_count // LANES
    return both[:half] * 64 + both[half:]


def widen(src_ref, dst_ref, step):
    @pl.loop(0, src_ref.shape[0] // step)
    def _(i):
        at = pl.ds(pl.multiple_of(i * step, step), step)
        dst_ref[at, :] = src_ref[at, :].astype(dst_ref.dtype)


def gather_kernel(owner_count, cap, index_ref, count_ref, table_ref, out_ref, wide, rows):
    widen(table_ref, wide, 256)

    @pl.loop(0, owner_count)
    def _(o):
        base = pl.multiple_of(o * cap, LANES)
        steps = (count_ref[o] + 15) // 16

        @pl.loop(0, steps)
        def _(i):
            for k in range(16):
                row = index_ref[base + i * 16 + k]
                rows[pl.ds(i * 16 + k, 1), :] = wide[pl.ds(row, 1), :]

        @pl.loop(0, steps)
        def _(i):
            at = pl.multiple_of(i * 16, 16)
            out_ref[pl.ds(pl.multiple_of(base + at, 16), 16), :] = rows[pl.ds(at, 16), :].astype(BF16)


def gather(index, count, table, owner_count, cap):
    return pl.pallas_call(
        functools.partial(gather_kernel, owner_count, cap),
        out_shape=jax.ShapeDtypeStruct((owner_count * cap, table.shape[1]), BF16),
        in_specs=[
            pl.BlockSpec(memory_space=SMEM),
            pl.BlockSpec(memory_space=SMEM),
            pl.BlockSpec(memory_space=VMEM),
        ],
        out_specs=pl.BlockSpec(memory_space=VMEM),
        scratch_shapes=[VMEM(table.shape, F32), VMEM((cap, table.shape[1]), F32)],
        compiler_params=pltpu.CompilerParams(vmem_limit_bytes=40 << 20),
        cost_estimate=pl.CostEstimate(flops=10**6, bytes_accessed=10**7, transcendentals=0),
    )(index, count, table)


def update_kernel(
    events, per_event, slot_ref, got_ref, code_ref, pick_ref, near_ref, gi_ref, gh_ref, bias_ref,
    rows_ref, new_ref, out_ref, wide, held,
):
    width = got_ref.shape[1]
    widen(got_ref, wide, 256)

    @pl.loop(0, slot_ref.shape[0] // 16)
    def _(i):
        for k in range(16):
            at = slot_ref[i * 16 + k]
            held[pl.ds(i * 16 + k, 1), :] = wide[pl.ds(at, 1), :]

    @pl.loop(0, events * (per_event - 1) // 256)
    def _(i):
        at = pl.ds(pl.multiple_of(events + i * 256, 256), 256)
        rows_ref[pl.ds(pl.multiple_of(i * 256, 256), 256), :] = held[at, :].astype(BF16)

    dest = held[:events, :].astype(BF16)
    wide_state = held[events * per_event :, :]
    dot = functools.partial(jnp.dot, preferred_element_type=F32)
    a = dot(dest, gi_ref[:width, :]) + dot(code_ref[...], gi_ref[width:, :]) + bias_ref[:, : 3 * width]
    b = dot(wide_state.astype(BF16), gh_ref[...])
    reset = jax.nn.sigmoid(a[:, :width] + b[:, :width])
    update = jax.nn.sigmoid(a[:, width : 2 * width] + b[:, width : 2 * width])
    cand = jnp.tanh(a[:, 2 * width :] + reset * (b[:, 2 * width :] + bias_ref[:, 3 * width :]))
    updated = ((1.0 - update) * cand + update * wide_state).astype(BF16)
    place = lax.broadcasted_iota(jnp.int32, (events, events), 1)
    chosen = (place == pick_ref[...]).astype(F32).astype(BF16)
    new_ref[...] = dot(chosen, updated).astype(BF16)
    slots = out_ref.shape[0]
    spot = lax.broadcasted_iota(jnp.int32, (slots, events), 0)
    out_ref[...] = dot((spot == near_ref[...]).astype(F32).astype(BF16), updated).astype(BF16)


def update(slot, got, code, pick, near_slot, gru_input, gru_hidden, bias, events, per_event, near_slots):
    width = got.shape[1]
    return pl.pallas_call(
        functools.partial(update_kernel, events, per_event),
        out_shape=(
            jax.ShapeDtypeStruct((events * (per_event - 1), width), BF16),
            jax.ShapeDtypeStruct((events, width), BF16),
            jax.ShapeDtypeStruct((near_slots, width), BF16),
        ),
        in_specs=[pl.BlockSpec(memory_space=SMEM)] + [pl.BlockSpec(memory_space=VMEM)] * 7,
        out_specs=(pl.BlockSpec(memory_space=VMEM),) * 3,
        scratch_shapes=[VMEM(got.shape, F32), VMEM((slot.shape[0], width), F32)],
        compiler_params=pltpu.CompilerParams(vmem_limit_bytes=48 << 20),
        cost_estimate=pl.CostEstimate(flops=10**6, bytes_accessed=10**7, transcendentals=0),
    )(slot, got, code, pick, near_slot, gru_input, gru_hidden, bias)


def attend_kernel(nb, rows_ref, code_ref, new_ref, grad_ref, wq_ref, wkv_ref, wm_ref, mb_ref, emb_ref, out_ref, kv, dkv):
    att = wq_ref.shape[1]
    mem = new_ref.shape[1]
    head = att // HEADS
    scale = 1.0 / math.sqrt(head)
    dot = functools.partial(jnp.dot, preferred_element_type=F32)
    same = (
        lax.broadcasted_iota(jnp.int32, (att, att), 0) // head
        == lax.broadcasted_iota(jnp.int32, (att, att), 1) // head
    ).astype(F32).astype(BF16)

    def head_sum(v):
        upper = v.astype(BF16)
        rest = (v - upper.astype(F32)).astype(BF16)
        return dot(upper, same) + dot(rest, same)

    def over_rows(x, y):
        return lax.dot_general(x, y, (((0,), (0,)), ((), ())), preferred_element_type=F32)

    new = new_ref[...]
    query = dot(new, wq_ref[...])
    scores = []
    for j in range(nb):
        kv[j] = dot(rows_ref[j], wkv_ref[:mem, :]) + dot(code_ref[j], wkv_ref[mem:, :])
        scores.append(head_sum(query * kv[j, :, :att]) * scale)
    top = functools.reduce(jnp.maximum, scores)
    shares = [jnp.exp(s - top) for s in scores]
    inverse = 1.0 / functools.reduce(jnp.add, shares)
    shares = [s * inverse for s in shares]
    mixed = functools.reduce(jnp.add, [shares[j] * kv[j, :, att:] for j in range(nb)]).astype(BF16)
    z = dot(mixed, wm_ref[:att, :]) + dot(new, wm_ref[att:, :]) + mb_ref[...]
    gate = 1.0 / (1.0 + jnp.exp(-z))
    emb_ref[...] = z * gate
    dz = grad_ref[...] * (gate * (1.0 + z * (1.0 - gate)))
    dz16 = dz.astype(BF16)
    dmixed = lax.dot_general(
        dz16, wm_ref[:att, :], (((1,), (1,)), ((), ())), preferred_element_type=F32
    ).astype(BF16).astype(F32)
    dshare = [head_sum(dmixed * kv[j, :, att:]) for j in range(nb)]
    mean = functools.reduce(jnp.add, [shares[j] * dshare[j] for j in range(nb)])
    dquery = jnp.zeros_like(query)
    for j in range(nb):
        dscore = shares[j] * (dshare[j] - mean) * scale
        dquery += dscore * kv[j, :, :att]
        dkv[j, :, :att] = (dscore * query).astype(BF16)
        dkv[j, :, att:] = (shares[j] * dmixed).astype(BF16)
    flat = dkv[...].reshape(-1, 2 * att)
    from_row = over_rows(rows_ref[...].reshape(-1, mem), flat)
    from_code = over_rows(code_ref[...].reshape(-1, code_ref.shape[2]), flat)

    @pl.when(pl.program_id(0) == 0)
    def _():
        out_ref[...] = jnp.zeros_like(out_ref)

    at = 0
    for piece in (
        over_rows(new, dquery.astype(BF16)),
        from_row[:, :att],
        from_code[:, :att],
        from_row[:, att:],
        from_code[:, att:],
        over_rows(mixed, dz16),
        over_rows(new, dz16),
    ):
        out_ref[at : at + piece.shape[0], :] += piece
        at += piece.shape[0]
    out_ref[at : at + 1, :] += jnp.sum(dz, axis=0, keepdims=True)


def attend(rows, code, new, out_grad, wq, wkv, wm, mb, packed_rows, block):
    nb, events, mem = rows.shape
    time = code.shape[2]
    att = wq.shape[1]
    whole = lambda a: pl.BlockSpec(a.shape, lambda i: (0,) * a.ndim)
    return pl.pallas_call(
        functools.partial(attend_kernel, nb),
        grid=(events // block,),
        out_shape=(
            jax.ShapeDtypeStruct(out_grad.shape, F32),
            jax.ShapeDtypeStruct((packed_rows, LANES), F32),
        ),
        in_specs=[
            pl.BlockSpec((nb, block, mem), lambda i: (0, i, 0)),
            pl.BlockSpec((nb, block, time), lambda i: (0, i, 0)),
            pl.BlockSpec((block, mem), lambda i: (i, 0)),
            pl.BlockSpec((block, mem), lambda i: (i, 0)),
            whole(wq),
            whole(wkv),
            whole(wm),
            whole(mb),
        ],
        out_specs=(
            pl.BlockSpec((block, mem), lambda i: (i, 0)),
            pl.BlockSpec((packed_rows, LANES), lambda i: (0, 0)),
        ),
        scratch_shapes=[VMEM((nb, block, 2 * att), F32), VMEM((nb, block, 2 * att), BF16)],
        compiler_params=pltpu.CompilerParams(vmem_limit_bytes=48 << 20),
        cost_estimate=pl.CostEstimate(flops=3 * 10**9, bytes_accessed=10**7, transcendentals=10**6),
    )(rows, code, new, out_grad, wq, wkv, wm, mb)


def write_kernel(senders, batches, cap, row_ref, count_ref, fresh_ref, table_ref, out_ref, wide, rows):
    widen(table_ref, wide, 256)
    widen(fresh_ref, rows, 256)

    @pl.loop(0, senders * batches)
    def _(order):
        block = lax.rem(order, batches) * senders + lax.div(order, batches)
        base = block * cap
        count = count_ref[block]

        @pl.loop(0, lax.div(count, 8))
        def _(i):
            for k in range(8):
                at = base + i * 8 + k
                wide[pl.ds(row_ref[at], 1), :] = rows[pl.ds(at, 1), :]

        @pl.loop(lax.div(count, 8) * 8, count)
        def _(i):
            wide[pl.ds(row_ref[base + i], 1), :] = rows[pl.ds(base + i, 1), :]

    widen(wide, out_ref, 256)


def write_back(row, count, fresh, table, senders, batches, cap):
    return pl.pallas_call(
        functools.partial(write_kernel, senders, batches, cap),
        out_shape=jax.ShapeDtypeStruct(table.shape, BF16),
        in_specs=[
            pl.BlockSpec(memory_space=SMEM),
            pl.BlockSpec(memory_space=SMEM),
            pl.BlockSpec(memory_space=VMEM),
            pl.BlockSpec(memory_space=VMEM),
        ],
        out_specs=pl.BlockSpec(memory_space=VMEM),
        scratch_shapes=[VMEM(table.shape, F32), VMEM(fresh.shape, F32)],
        compiler_params=pltpu.CompilerParams(vmem_limit_bytes=40 << 20),
        cost_estimate=pl.CostEstimate(flops=10**6, bytes_accessed=10**7, transcendentals=0),
    )(row, count, fresh, table)


def on_device(
    memory, src_owner, src_row, fetch_owner, fetch_row, event_tick, source_tick, neighbour_tick,
    time_freq, time_phase, gru_input, gru_hidden, gru_bias, w_query, w_kv, w_merge, merge_bias, out_grad,
):
    owner_count = lax.axis_size("node")
    batch_count = lax.axis_size("batch")
    events = src_row.shape[0]
    per_event = fetch_row.shape[1]
    mem = memory.shape[1]
    att = w_query.shape[1]
    time = time_freq.shape[0]
    near_cap = events * 2 // owner_count
    cap = near_cap * (per_event + 1)
    to_all = functools.partial(lax.all_to_all, axis_name="node", split_axis=0, concat_axis=0, tiled=True)

    near_owner = src_owner[:, 0]
    owners = jnp.concatenate([fetch_owner[:, :, 0].T, near_owner[None]], 0).reshape(-1, LANES)
    wanted = jnp.concatenate([fetch_row.T, src_row[None]], 0).reshape(-1)
    slot = (owners * cap + ranks(owners, owner_count)).reshape(-1)
    ask = spread(slot, wanted, owner_count * cap).reshape(owner_count, cap)
    got = to_all(ask)
    count = jnp.sum((got > 0).astype(jnp.int32), axis=1)
    index = jnp.maximum(got - 1, 0).reshape(-1)
    sent = gather(index, count, memory, owner_count, cap)
    back = to_all(sent.reshape(owner_count, cap, mem)).reshape(-1, mem)

    near_grid = near_owner.reshape(-1, LANES)
    near_slot = (near_grid * near_cap + ranks(near_grid, owner_count)).reshape(-1)
    near_ask = spread(near_slot, src_row, owner_count * near_cap).reshape(owner_count, near_cap)
    near_got = lax.all_gather(to_all(near_ask), "batch", axis=0, tiled=True)
    near_count = jnp.sum((near_got > 0).astype(jnp.int32), axis=1)
    near_row = jnp.maximum(near_got - 1, 0).reshape(-1)

    same = (near_owner[:, None] == near_owner[None, :]) & (src_row[:, None] == src_row[None, :])
    places = jnp.arange(events, dtype=jnp.int32)
    pick = jnp.max(jnp.where(same, places[None, :], jnp.int32(-1)), axis=1, keepdims=True)
    source_code = cos_code((event_tick - source_tick).astype(F32), time_freq, time_phase)
    nb_code = cos_code((event_tick[None, :] - neighbour_tick.T).astype(F32), time_freq, time_phase)

    kv_rows, new_src, outgoing = update(
        slot, back, source_code, pick, near_slot[None, :], gru_input, gru_hidden, gru_bias[None, :],
        events, per_event, owner_count * near_cap,
    )
    arrived = to_all(outgoing.reshape(owner_count, near_cap, mem))
    fresh = lax.all_gather(arrived, "batch", axis=0, tiled=True).reshape(-1, mem)
    used = att + 2 * (mem + time) + att + mem
    embedding, packed = attend(
        kv_rows.reshape(per_event - 1, events, mem), nb_code, new_src, out_grad,
        w_query, w_kv, w_merge, merge_bias[None, :], used + 8, 256,
    )
    total = lax.psum(packed, ("node", "batch"))
    memory_out = write_back(near_row, near_count, fresh, memory, owner_count, batch_count, near_cap)
    kv_end = mem + 2 * (mem + time)
    grad_kv = jnp.concatenate([total[mem : mem + mem + time], total[mem + mem + time : kv_end]], axis=1)
    return embedding, memory_out, total[:mem], grad_kv, total[kv_end:used], total[used]


def solution(mesh):
    both = ("node", "batch")
    return jax.shard_map(
        on_device,
        mesh=mesh,
        in_specs=(
            P("node", None), P(both, None), P(both), P(both, None, None), P(both, None),
            P(both), P(both), P(both, None),
            P(), P(), P(), P(), P(), P(), P(), P(), P(),
            P(both, None),
        ),
        out_specs=(P(both, None), P("node", None), P(), P(), P(), P()),
        check_vma=False,
    )
```

time: 349 us -> 262 us (0.75)
  local copies, waits for them, and re-layouts: 140 us -> 11.5 us
  waiting for transfers between devices: 49.7 us -> 137 us
  other arithmetic: 51.1 us -> 7.47 us
  Pallas kernels: 0 us -> 37.2 us
  blocking collectives: 65.1 us -> 41.4 us
  starting transfers between devices: 16.3 us -> 8.53 us
  matrix products: 9.36 us -> 1.65 us
    gather x6 -> x0, local copies, waits for them, and re-layouts: 82.1 us -> none  [the longest x1 39.8 us: on_device(): far_rows = memory[far_got]]
    psum x1, waiting for transfers between devices: 28.8 us -> 104 us  [on_device(): total = lax.psum(packed, ('node', 'batch'))]
    psum x1 -> x0, blocking collectives: 41.7 us -> none  [on_device(): lax.psum((grads[0], grads[1], grads[2], grads[3]), ('node', 'batch'))]
    pallas_call x0 -> x4, Pallas kernels: none -> 37.2 us  [the longest x1 11.4 us: attend(): pl.pallas_call(functools.partial(attend_kernel, nb), grid=(events // bloc...]
    scatter x3 -> x0, local copies, waits for them, and re-layouts: 36.6 us -> none  [the longest x1 21.1 us: on_device(): far_ask = jnp.zeros((owner_count * far_cap,), jnp.int32).at[far_slot].set...]
    another operation x5 -> x0, other arithmetic: 27.2 us -> none  [the longest x1 23.5 us: on_device(): best = jnp.full((node_local + 1,), -1, jnp.int32).at[key_rows].max(all_keys)]
    all_to_all x1 -> x3, blocking collectives: 9.88 us -> 28.2 us  [the longest x1 11.3 us: on_device(): arrived = to_all(outgoing.reshape(owner_count, near_cap, mem))]
    all_to_all x4 -> x1, waiting for transfers between devices: 20.9 us -> 33.4 us  [on_device(): back = to_all(sent.reshape(owner_count, cap, mem)).reshape(-1, mem)]
  transfers between devices with their start and end apart: 6 -> 3, of which waited for: 3 -> 2; matrix products, arithmetic and copies ran while one was open for 35% -> 4% of each run, Pallas kernels for 0% -> 0%
where the time goes in v1:
time: 262 us; the launch traced here: 261 us
  waiting for transfers between devices  137 us (52%)
  blocking collectives  41.4 us (16%)
  Pallas kernels  37.2 us (14%)
  between operations  15.9 us (6%)
  local copies, waits for them, and re-layouts  11.5 us (4%)
  starting transfers between devices  8.53 us (3%)
  other arithmetic  7.47 us (3%)
    psum x1, waiting for transfers between devices, on_device(): total = lax.psum(packed, ('node', 'batch'))  104 us
    all_to_all x1, waiting for transfers between devices, on_device(): back = to_all(sent.reshape(owner_count, cap, mem)).reshape(-1, mem)  33.4 us
    all_gather x1, blocking collectives, on_device(): near_got = lax.all_gather(to_all(near_ask), 'batch', axis=0, tiled=True)  13.2 us
    pallas_call x1, Pallas kernels, attend(): pl.pallas_call(functools.partial(attend_kernel, nb), grid=(events // bloc...  11.4 us
    all_to_all x1, blocking collectives, on_device(): arrived = to_all(outgoing.reshape(owner_count, near_cap, mem))  11.3 us
    all_to_all x1, blocking collectives, on_device(): got = to_all(ask)  9.89 us
    pallas_call x1, Pallas kernels, update(): pl.pallas_call(functools.partial(update_kernel, events, per_event), out_s...  9.57 us
    pallas_call x1, Pallas kernels, gather(): pl.pallas_call(functools.partial(gather_kernel, owner_count, cap), out_sh...  8.88 us
  transfers between devices with their start and end apart: 3, of which 2 were waited for; matrix products, arithmetic and copies ran while one was open for 4% of the time, Pallas kernels for 0%

profile of v1, /device:TPU:0, one launch (start us, length us, event | category | flops | bytes accessed | tf_op | source)
XLA Modules:
  0.0 260.7 jit_solution(4495776206905335395)
XLA Ops:
  8.0 0.7 copy.36
  8.7 0.7 broadcast_multiply_fusion
  9.4 0.1 fusion.15
  9.6 0.1 fusion.39
  9.7 0.2 fusion.7
  9.9 0.8 add_add_fusion
  10.8 0.0 copy-start.6
  10.8 0.6 copy-done.6
  11.4 0.4 select_convert_fusion.1
  11.8 0.8 fusion.8
  12.7 9.9 %all_to_all.31 = s32[8,1,1536]{2,1,0:T(1,128)S(1)} all-to-all(s32[8,1,1536]{2,1,0:T(1,128)S(1)} %bitcast.54), channel_id=1, replica_groups=mesh['node'=8,'batch'=4] {'node'}, dimensions={0} | all-to-all | bytes 98304 | tf_op jit(solution)/shard_map/all_to_all | solution.py:311
  22.6 0.3 fusion.19
  22.8 8.9 %shard_map.217 = bf16[12288,128]{1,0:T(8,128)(2,1)S(1)} custom-call(s32[12288]{0:T(1024)S(1)} %bitcast.49, s32[8]{0:T(128)S(1)} %get-tuple-element.23.count_ref, bf16[8192,128]{1,0:T(8,128)(2,1)S(1)} %copy-done.1), custom_call_target="tpu_custom_call" | custom-call | flops 1000000 | bytes 10000000 | tf_op jit(solution)/shard_map/pallas_call | solution.py:83
  31.7 1.6 copy-done
  33.4 0.0 copy-start.17
  33.4 0.0 copy-start.10
  33.4 8.5 %all-to-all-start.1 = ((bf16[8,1536,128]{2,1,0:T(8,128)(2,1)}), bf16[8,1536,128]{2,1,0:T(8,128)(2,1)S(1)}, u32[]{:S(2)}, u32[]{:S(2)}) async-start(bf16[8,1536,128]{2,1,0:T(8,128)(2,1)} %bitcast.46), calls=%async_computation.1 | async-start | bytes 6291456 | tf_op jit(solution)/shard_map/all_to_all | solution.py:315
  41.9 0.0 all-reduce.2.cloned.1.call-start
  41.9 0.1 fusion.41
  42.0 0.2 fusion.50
  42.2 0.2 fusion.12
  42.3 0.0 copy-start.21
  42.4 0.4 select_reduce_fusion
  42.8 0.1 copy.32.pick_ref
  43.0 0.3 add_convert_fusion.1.code_ref
  43.3 0.0 copy-start.15
  43.3 3.0 %add_convert_fusion.code_ref = bf16[10,512,128]{2,1,0:T(8,128)(2,1)} fusion(f32[128]{0:T(128)S(1)} %get-tuple-element.39, f32[128]{0:T(128)S(1)} %get-tuple-element.40, f32[10,512]{1,0:T(8,128)S(1)} %convert_bitcast_fusion), kind=kLoop, calls=%fused_computation.4 | loop fusion | flops 14417920 | bytes 1332224 | tf_op jit(solution)/shard_map/convert_element_type | solution.py:27
  46.3 33.4 %all-to-all-done.1 = bf16[8,1536,128]{2,1,0:T(8,128)(2,1)S(1)} async-done(((bf16[8,1536,128]{2,1,0:T(8,128)(2,1)}), bf16[8,1536,128]{2,1,0:T(8,128)(2,1)S(1)}, u32[]{:S(2)}, u32[]{:S(2)}) %all-to-all-start.1) | async-done | bytes 3145760 | tf_op jit(solution)/shard_map/all_to_all | solution.py:315
  79.8 0.8 copy-done.7
  80.6 0.9 copy-done.8
  81.5 0.9 copy-done.9
  82.4 9.6 %shard_map.218 = (bf16[5120,128]{1,0:T(8,128)(2,1)S(1)}, bf16[512,128]{1,0:T(8,128)(2,1)S(1)}, bf16[1024,128]{1,0:T(8,128)(2,1)S(1)}) custom-call(s32[6144]{0:T(1024)S(1)} %copy-done.7, bf16[12288,128]{1,0:T(8,128)(2,1)S(1)} %bitcast.45, bf16[512,128]{1,0:T(8,128)(2,1)S(1)} %add_convert_fusion.1.code_ref, s32[512,1]{1,0:T(8,128)S(1)} %copy.32.pick_ref, ...), custom_call_target="tpu_custom_call" | custom-call | flops 1000000 | bytes 10000000 | tf_op jit(solution)/shard_map/pallas_call | solution.py:135
  92.1 11.4 %shard_map.219 = (f32[512,128]{1,0:T(8,128)}, f32[904,128]{1,0:T(8,128)}) custom-call(bf16[10,512,128]{2,1,0:T(8,128)(2,1)S(1)} %bitcast.52, bf16[10,512,128]{2,1,0:T(8,128)(2,1)S(1)} %copy-done.3, bf16[512,128]{1,0:T(8,128)(2,1)S(1)} %get-tuple-element.12.new_ref, f32[512,128]{1,0:T(8,128)S(1)} %copy-done.11, bf16[128,128]{1,0:T(8,128)(2,1)S(1)} %copy-done.14, ...), custom_call_target="tpu_custom_call" | custom-call | flops 3000000000 | bytes 10000000 | tf_op jit(solution)/shard_map/pallas_call | solution.py:224
  103.5 0.0 all-reduce.2.cloned.1.call-update
  103.5 0.0 all-gather.3.cloned.1.call-start
  103.6 11.3 %all_to_all.32 = bf16[8,128,128]{2,1,0:T(8,128)(2,1)} all-to-all(bf16[8,128,128]{2,1,0:T(8,128)(2,1)} %bitcast.48), channel_id=1, replica_groups=mesh['node'=8,'batch'=4] {'node'}, dimensions={0} | all-to-all | bytes 524288 | tf_op jit(solution)/shard_map/all_to_all | solution.py:334
  114.8 0.0 all-gather.3.cloned.1.call-update
  114.9 0.2 convolution_convert_fusion
  115.1 7.0 %all_to_all.33 = s32[8,1,128]{2,1,0:T(1,128)S(1)} all-to-all(s32[8,1,128]{2,1,0:T(1,128)S(1)} %bitcast.63), channel_id=1, replica_groups=mesh['node'=8,'batch'=4] {'node'}, dimensions={0} | all-to-all | bytes 8192 | tf_op jit(solution)/shard_map/all_to_all | solution.py:320
  122.1 13.2 %all-gather = s32[32,1,128]{2,1,0:T(1,128)S(1)} all-gather(s32[8,1,128]{2,1,0:T(1,128)S(1)} %all_to_all.33), channel_id=2, replica_groups=mesh['node'=8,'batch'=4] {'batch'}, dimensions={0}, use_global_device_ids=true | all-gather | bytes 20480 | tf_op jit(solution)/shard_map/all_gather | solution.py:320
  135.3 0.7 fusion.28
  136.0 103.6 %all-reduce.2.cloned.1.call-done = f32[904,128]{1,0:T(8,128)} async-done(((f32[904,128]{1,0:T(8,128)}), f32[904,128]{1,0:T(8,128)}) %all-reduce.2.cloned.1.call-update) | async-done | bytes 462864 | tf_op jit(solution)/shard_map/psum | solution.py:341
  239.6 1.5 slice.40
  241.0 1.7 fusion.64
  242.7 0.7 pad_maximum_fusion
  243.5 1.2 slice_bitcast_fusion
  244.7 1.2 copy-done.4
  245.9 7.3 %shard_map.220 = bf16[8192,128]{1,0:T(8,128)(2,1)} custom-call(s32[4096]{0:T(1024)S(1)} %bitcast.50, s32[32]{0:T(128)S(1)} %get-tuple-element.29.count_ref, bf16[4096,128]{1,0:T(8,128)(2,1)S(1)} %bitcast.47, bf16[8192,128]{1,0:T(8,128)(2,1)S(1)} %copy-done.2), custom_call_target="tpu_custom_call" | custom-call | flops 1000000 | bytes 10000000 | tf_op jit(solution)/shard_map/pallas_call | solution.py:275
  (56 shorter events, 0.2 us)
Async XLA Ops:
  10.8 0.6 copy-start.6
  11.8 11.0 %copy-start.1 = (bf16[8192,128]{1,0:T(8,128)(2,1)S(1)}, bf16[8192,128]{1,0:T(8,128)(2,1)}, u32[]{:S(2)}) copy-start(bf16[8192,128]{1,0:T(8,128)(2,1)} %table_ref.3) | copy-start | bytes 6291460
  31.7 1.7 copy-start
  33.3 8.6 %copy-start.16 = (s32[512,1]{0,1:T(1,128)S(1)}, s32[512,1]{0,1:T(1,128)}, u32[]{:S(2)}) copy-start(s32[512,1]{0,1:T(1,128)} %param.19) | copy-start | bytes 6148
  33.4 9.0 %copy-start.18 = (s32[512]{0:T(512)S(1)}, s32[512]{0:T(512)}, u32[]{:S(2)}) copy-start(s32[512]{0:T(512)} %param.20) | copy-start | bytes 6148
  33.4 9.6 %copy-start.24 = (f32[128]{0:T(128)S(1)}, f32[128]{0:T(128)}, u32[]{:S(2)}) copy-start(f32[128]{0:T(128)} %param.27) | copy-start | bytes 1540
  33.4 9.6 %copy-start.25 = (f32[128]{0:T(128)S(1)}, f32[128]{0:T(128)}, u32[]{:S(2)}) copy-start(f32[128]{0:T(128)} %param.26) | copy-start | bytes 1540
  33.4 9.6 %copy-start.20 = (s32[512]{0:T(512)S(1)}, s32[512]{0:T(512)}, u32[]{:S(2)}) copy-start(s32[512]{0:T(512)} %param.23) | copy-start | bytes 6148
  33.4 9.6 %copy-start.23 = (s32[512]{0:T(512)S(1)}, s32[512]{0:T(512)}, u32[]{:S(2)}) copy-start(s32[512]{0:T(512)} %param.24) | copy-start | bytes 6148
  33.4 9.6 %copy-start.17 = (s32[512,10]{0,1:T(8,128)S(1)}, s32[512,10]{0,1:T(8,128)}, u32[]{:S(2)}) copy-start(s32[512,10]{0,1:T(8,128)} %param.25) | copy-start | bytes 61444
  33.4 46.4 %copy-start.10 = (f32[512]{0:T(512)S(1)}, f32[512]{0:T(512)}, u32[]{:S(2)}) copy-start(f32[512]{0:T(512)} %param.30) | copy-start | bytes 6148
  33.4 46.3 %all-to-all-start.1 = ((bf16[8,1536,128]{2,1,0:T(8,128)(2,1)}), bf16[8,1536,128]{2,1,0:T(8,128)(2,1)S(1)}, u32[]{:S(2)}, u32[]{:S(2)}) async-start(bf16[8,1536,128]{2,1,0:T(8,128)(2,1)} %bitcast.46), calls=%async_computation.1 | async-start | bytes 6291456 | tf_op jit(solution)/shard_map/all_to_all | solution.py:315
  41.9 197.7 %all-reduce.2.cloned.1.call-start = ((), (), s32[]{:S(2)}) async-start(), calls=%async_computation.5 | async-start | bytes 925696 | tf_op jit(solution)/shard_map/psum | solution.py:341
  42.3 0.7 copy-start.21
  43.3 48.7 %copy-start.15 = (f32[128]{0:T(128)S(1)}, f32[128]{0:T(128)}, u32[]{:S(2)}) copy-start(f32[128]{0:T(128)} %param.34) | copy-start | bytes 1540
  79.7 12.3 %copy-start.3 = (bf16[10,512,128]{2,1,0:T(8,128)(2,1)S(1)}, bf16[10,512,128]{2,1,0:T(8,128)(2,1)}, u32[]{:S(2)}) copy-start(bf16[10,512,128]{2,1,0:T(8,128)(2,1)} %add_convert_fusion.code_ref) | copy-start | bytes 3932164
  79.7 0.8 copy-start.7
  80.6 0.9 copy-start.8
  81.5 0.9 copy-start.9
  82.4 9.6 %copy-start.11 = (f32[512,128]{1,0:T(8,128)S(1)}, f32[512,128]{1,0:T(8,128)}, u32[]{:S(2)}) copy-start(f32[512,128]{1,0:T(8,128)} %grad_ref.1) | copy-start | bytes 786436
  82.4 9.6 %copy-start.12 = (bf16[256,256]{1,0:T(8,128)(2,1)S(1)}, bf16[256,256]{1,0:T(8,128)(2,1)}, u32[]{:S(2)}) copy-start(bf16[256,256]{1,0:T(8,128)(2,1)} %wkv_ref.1) | copy-start | bytes 393220
  82.4 9.6 %copy-start.13 = (bf16[256,128]{1,0:T(8,128)(2,1)S(1)}, bf16[256,128]{1,0:T(8,128)(2,1)}, u32[]{:S(2)}) copy-start(bf16[256,128]{1,0:T(8,128)(2,1)} %wm_ref.1) | copy-start | bytes 196612
  82.4 9.6 %copy-start.14 = (bf16[128,128]{1,0:T(8,128)(2,1)S(1)}, bf16[128,128]{1,0:T(8,128)(2,1)}, u32[]{:S(2)}) copy-start(bf16[128,128]{1,0:T(8,128)(2,1)} %wq_ref.1) | copy-start | bytes 98308
  92.0 11.5 %copy-start.5 = (bf16[1024,128]{1,0:T(8,128)(2,1)}, bf16[1024,128]{1,0:T(8,128)(2,1)S(1)}, u32[]{:S(2)}) copy-start(bf16[1024,128]{1,0:T(8,128)(2,1)S(1)} %get-tuple-element.14) | copy-start | bytes 786436
  92.1 22.8 %copy-start.19 = (s32[512]{0:T(512)S(1)}, s32[512]{0:T(512)}, u32[]{:S(2)}) copy-start(s32[512]{0:T(512)} %param.20) | copy-start | bytes 6148
  92.1 22.8 %copy-start.22 = (f32[4,128]{1,0:T(4,128)S(1)}, f32[4,128]{1,0:T(4,128)}, u32[]{:S(2)}) copy-start(f32[4,128]{1,0:T(4,128)} %copy-done.21) | copy-start | bytes 6148
  103.5 141.2 %copy-start.2 = (bf16[8192,128]{1,0:T(8,128)(2,1)S(1)}, bf16[8192,128]{1,0:T(8,128)(2,1)}, u32[]{:S(2)}) copy-start(bf16[8192,128]{1,0:T(8,128)(2,1)} %table_ref.3) | copy-start | bytes 6291460
  103.5 141.1 %all-gather.3.cloned.1.call-start = ((), (), s32[]{:S(2)}) async-start(), calls=%async_computation.4 | async-start | bytes 1310720 | tf_op jit(solution)/shard_map/all_gather | solution.py:335
  244.7 1.2 copy-start.4
Sparse Core Ops, SparseCore 0:
  103.6 135.8 all-reduce.1
Sparse Core Ops, SparseCore 1:
  115.0 27.7 all-gather.2

commit v2 on v1

--- a/solution.py
+++ b/solution.py
@@ -308,16 +308,17 @@
     wanted = jnp.concatenate([fetch_row.T, src_row[None]], 0).reshape(-1)
     slot = (owners * cap + ranks(owners, owner_count)).reshape(-1)
     ask = spread(slot, wanted, owner_count * cap).reshape(owner_count, cap)
-    got = to_all(ask)
+    near_grid = near_owner.reshape(-1, LANES)
+    near_slot = (near_grid * near_cap + ranks(near_grid, owner_count)).reshape(-1)
+    near_ask = spread(near_slot, src_row, owner_count * near_cap).reshape(owner_count, near_cap)
+    asked = to_all(jnp.concatenate([ask, near_ask], axis=1))
+    got = asked[:, :cap]
     count = jnp.sum((got > 0).astype(jnp.int32), axis=1)
     index = jnp.maximum(got - 1, 0).reshape(-1)
     sent = gather(index, count, memory, owner_count, cap)
     back = to_all(sent.reshape(owner_count, cap, mem)).reshape(-1, mem)
 
-    near_grid = near_owner.reshape(-1, LANES)
-    near_slot = (near_grid * near_cap + ranks(near_grid, owner_count)).reshape(-1)
-    near_ask = spread(near_slot, src_row, owner_count * near_cap).reshape(owner_count, near_cap)
-    near_got = lax.all_gather(to_all(near_ask), "batch", axis=0, tiled=True)
+    near_got = lax.all_gather(asked[:, cap:], "batch", axis=0, tiled=True)
     near_count = jnp.sum((near_got > 0).astype(jnp.int32), axis=1)
     near_row = jnp.maximum(near_got - 1, 0).reshape(-1)
 
@@ -334,11 +335,15 @@
     arrived = to_all(outgoing.reshape(owner_count, near_cap, mem))
     fresh = lax.all_gather(arrived, "batch", axis=0, tiled=True).reshape(-1, mem)
     used = att + 2 * (mem + time) + att + mem
+    devices = owner_count * batch_count
+    packed_rows = -(-(used + 1) // (8 * devices)) * 8 * devices
     embedding, packed = attend(
         kv_rows.reshape(per_event - 1, events, mem), nb_code, new_src, out_grad,
-        w_query, w_kv, w_merge, merge_bias[None, :], used + 8, 256,
+        w_query, w_kv, w_merge, merge_bias[None, :], packed_rows, 256,
     )
-    total = lax.psum(packed, ("node", "batch"))
+    both = ("node", "batch")
+    parts = lax.all_to_all(packed.reshape(devices, -1, LANES), both, split_axis=0, concat_axis=0, tiled=True)
+    total = lax.all_gather(jnp.sum(parts, axis=0), both, axis=0, tiled=True)
     memory_out = write_back(near_row, near_count, fresh, memory, owner_count, batch_count, near_cap)
     kv_end = mem + 2 * (mem + time)
     grad_kv = jnp.concatenate([total[mem : mem + mem + time], total[mem + mem + time : kv_end]], axis=1)

time: 262 us -> 233 us (0.89)
  waiting for transfers between devices: 137 us -> 34.6 us
  blocking collectives: 41.4 us -> 100 us
  starting transfers between devices: 8.53 us -> 16.6 us
  local copies, waits for them, and re-layouts: 11.5 us -> 19.4 us
    psum x1 -> x0, waiting for transfers between devices: 104 us -> none  [on_device(): total = lax.psum(packed, ('node', 'batch'))]
    all_gather x1 -> x2, blocking collectives: 13.2 us -> 90.1 us  [the longest x1 69.3 us: on_device(): total = lax.all_gather(jnp.sum(parts, axis=0), both, axis=0, tiled=True)]
    all_to_all x3 -> x1, blocking collectives: 28.2 us -> 9.92 us  [on_device(): asked = to_all(jnp.concatenate([ask, near_ask], axis=1))]
    all_to_all x0 -> x2, starting transfers between devices: none -> 10.1 us  [the longest x1 6.73 us: on_device(): lax.all_to_all(packed.reshape(devices, -1, LANES), both, split_axis=0, co...]
    unnamed x53 -> x60, local copies, waits for them, and re-layouts: 6.97 us -> 16.7 us
  transfers between devices with their start and end apart: 3 -> 4, of which waited for: 2 -> 1; matrix products, arithmetic and copies ran while one was open for 4% -> 3% of each run, Pallas kernels for 0% -> 5%
where the time goes in v2:
time: 233 us; the launch traced here: 232 us
  blocking collectives  100 us (43%)
  Pallas kernels  38.4 us (16%)
  waiting for transfers between devices  34.6 us (15%)
  local copies, waits for them, and re-layouts  19.4 us (8%)
  starting transfers between devices  16.6 us (7%)
  between operations  14.4 us (6%)
  other arithmetic  6.9 us (3%)
    all_gather x1, blocking collectives, on_device(): total = lax.all_gather(jnp.sum(parts, axis=0), both, axis=0, tiled=True)  69.3 us
    all_to_all x1, waiting for transfers between devices, on_device(): back = to_all(sent.reshape(owner_count, cap, mem)).reshape(-1, mem)  33.9 us
    all_gather x1, blocking collectives, on_device(): near_got = lax.all_gather(asked[:, cap:], 'batch', axis=0, tiled=True)  20.8 us
    unnamed x60, local copies, waits for them, and re-layouts  16.7 us
    pallas_call x1, Pallas kernels, attend(): pl.pallas_call(functools.partial(attend_kernel, nb), grid=(events // bloc...  11.4 us
    all_to_all x1, blocking collectives, on_device(): asked = to_all(jnp.concatenate([ask, near_ask], axis=1))  9.92 us
    pallas_call x1, Pallas kernels, gather(): pl.pallas_call(functools.partial(gather_kernel, owner_count, cap), out_sh...  9.84 us
    pallas_call x1, Pallas kernels, update(): pl.pallas_call(functools.partial(update_kernel, events, per_event), out_s...  9.56 us
  transfers between devices with their start and end apart: 4, of which 1 were waited for; matrix products, arithmetic and copies ran while one was open for 3% of the time, Pallas kernels for 5%

profile of v2, /device:TPU:0, one launch (start us, length us, event | category | flops | bytes accessed | tf_op | source)
XLA Modules:
  0.0 232.0 jit_solution(8249171784142665445)
XLA Ops:
  7.2 0.7 copy.32
  7.9 0.7 broadcast_multiply_fusion
  8.6 0.1 fusion.15
  8.9 0.2 fusion.7
  9.1 0.8 add_add_fusion
  10.0 0.6 copy-done.6
  10.6 0.4 select_convert_fusion.1
  11.0 0.8 fusion.8
  12.0 0.2 fusion.48
  12.2 0.2 fusion.12
  12.4 0.2 convolution_convert_fusion
  12.6 9.9 %all_to_all.27 = s32[8,1,1664]{2,1,0:T(1,128)S(1)} all-to-all(s32[8,1,1664]{2,1,0:T(1,128)S(1)} %all_to_all.17), channel_id=1, replica_groups=mesh['node'=8,'batch'=4] {'node'}, dimensions={0} | all-to-all | bytes 106496 | tf_op jit(solution)/shard_map/all_to_all | solution.py:314
  22.6 0.5 copy-done.21
  23.1 9.8 %shard_map.217 = bf16[12288,128]{1,0:T(8,128)(2,1)S(1)} custom-call(s32[12288]{0:T(1024)S(1)} %reshape.213.index_ref, s32[8]{0:T(128)S(1)} %get-tuple-element.23.count_ref, bf16[8192,128]{1,0:T(8,128)(2,1)S(1)} %copy-done.1), custom_call_target="tpu_custom_call" | custom-call | flops 1000000 | bytes 10000000 | tf_op jit(solution)/shard_map/pallas_call | solution.py:83
  33.0 1.6 copy-done
  34.7 6.4 %all-to-all-start.1 = ((bf16[8,1536,128]{2,1,0:T(8,128)(2,1)}), bf16[8,1536,128]{2,1,0:T(8,128)(2,1)S(1)}, u32[]{:S(2)}, u32[]{:S(2)}) async-start(bf16[8,1536,128]{2,1,0:T(8,128)(2,1)} %bitcast.46), calls=%async_computation.1 | async-start | bytes 6291456 | tf_op jit(solution)/shard_map/all_to_all | solution.py:319
  41.1 0.4 select_reduce_fusion
  41.5 0.1 copy.26.pick_ref
  41.8 0.3 add_convert_fusion.1.code_ref
  42.0 3.0 %add_convert_fusion.code_ref = bf16[10,512,128]{2,1,0:T(8,128)(2,1)} fusion(f32[128]{0:T(128)S(1)} %get-tuple-element.41, f32[128]{0:T(128)S(1)} %get-tuple-element.42, f32[10,512]{1,0:T(8,128)S(1)} %convert_bitcast_fusion), kind=kLoop, calls=%fused_computation.4 | loop fusion | flops 14417920 | bytes 1332224 | tf_op jit(solution)/shard_map/convert_element_type | solution.py:27
  45.1 33.9 %all-to-all-done.1 = bf16[8,1536,128]{2,1,0:T(8,128)(2,1)S(1)} async-done(((bf16[8,1536,128]{2,1,0:T(8,128)(2,1)}), bf16[8,1536,128]{2,1,0:T(8,128)(2,1)S(1)}, u32[]{:S(2)}, u32[]{:S(2)}) %all-to-all-start.1) | async-done | bytes 3145760 | tf_op jit(solution)/shard_map/all_to_all | solution.py:319
  79.0 0.7 copy-done.7
  79.7 0.9 copy-done.8
  80.7 0.9 copy-done.9
  81.5 9.6 %shard_map.218 = (bf16[5120,128]{1,0:T(8,128)(2,1)S(1)}, bf16[512,128]{1,0:T(8,128)(2,1)S(1)}, bf16[1024,128]{1,0:T(8,128)(2,1)S(1)}) custom-call(s32[6144]{0:T(1024)S(1)} %copy-done.7, bf16[12288,128]{1,0:T(8,128)(2,1)S(1)} %bitcast.45, bf16[512,128]{1,0:T(8,128)(2,1)S(1)} %add_convert_fusion.1.code_ref, s32[512,1]{1,0:T(8,128)S(1)} %copy.26.pick_ref, ...), custom_call_target="tpu_custom_call" | custom-call | flops 1000000 | bytes 10000000 | tf_op jit(solution)/shard_map/pallas_call | solution.py:135
  91.1 0.7 copy-done.5
  91.8 1.1 copy-done.11
  92.9 0.7 copy-done.15
  93.5 3.4 %all-to-all-start.2 = ((bf16[8,128,128]{2,1,0:T(8,128)(2,1)}), bf16[8,128,128]{2,1,0:T(8,128)(2,1)S(1)}, u32[]{:S(2)}, u32[]{:S(2)}) async-start(bf16[8,128,128]{2,1,0:T(8,128)(2,1)} %bitcast.48), calls=%async_computation.2 | async-start | bytes 524288 | tf_op jit(solution)/shard_map/all_to_all | solution.py:335
  97.0 1.3 copy-done.3
  98.3 1.3 copy-done.12
  99.6 0.9 copy-done.13
  100.5 0.9 copy-done.14
  101.5 0.9 copy-done.16
  102.4 0.8 copy-done.17
  103.2 0.8 copy-done.18
  104.0 11.4 %shard_map.219 = (f32[512,128]{1,0:T(8,128)}, f32[1024,128]{1,0:T(8,128)}) custom-call(bf16[10,512,128]{2,1,0:T(8,128)(2,1)S(1)} %bitcast.50, bf16[10,512,128]{2,1,0:T(8,128)(2,1)S(1)} %copy-done.3, bf16[512,128]{1,0:T(8,128)(2,1)S(1)} %copy-done.16, f32[512,128]{1,0:T(8,128)S(1)} %copy-done.13, bf16[128,128]{1,0:T(8,128)(2,1)S(1)} %copy-done.18, ...), custom_call_target="tpu_custom_call" | custom-call | flops 3000000000 | bytes 10000000 | tf_op jit(solution)/shard_map/pallas_call | solution.py:224
  115.4 6.7 %all-to-all-start.3 = ((f32[32,32,128]{2,1,0:T(8,128)}), f32[32,32,128]{2,1,0:T(8,128)S(1)}, u32[]{:S(2)}, u32[]{:S(2)}) async-start(f32[32,32,128]{2,1,0:T(8,128)} %bitcast.20), calls=%async_computation.3 | async-start | bytes 1048576 | tf_op jit(solution)/shard_map/all_to_all | solution.py:345
  122.2 0.7 all-gather.2.cloned.1.call-update
  122.8 0.7 slice.49
  123.5 20.8 %all_gather.9 = s32[32,128]{1,0:T(8,128)S(1)} all-gather(s32[8,128]{1,0:T(8,128)S(1)} %slice.49), channel_id=1, replica_groups=mesh['node'=8,'batch'=4] {'batch'}, dimensions={0}, use_global_device_ids=true | all-gather | bytes 20480 | tf_op jit(solution)/shard_map/all_gather | solution.py:321
  144.5 69.3 %all_gather.11 = f32[1024,128]{1,0:T(8,128)S(1)} all-gather(f32[32,128]{1,0:T(8,128)S(1)} %reduce_sum.75), channel_id=1, replica_groups=mesh['node'=8,'batch'=4] {'node','batch'}, dimensions={0}, use_global_device_ids=true | all-gather | bytes 540672 | tf_op jit(solution)/shard_map/all_gather | solution.py:346
  213.8 0.6 slice.50
  214.5 0.7 fusion.62
  215.1 0.7 pad_maximum_fusion
  215.9 0.5 slice_bitcast_fusion
  216.4 1.2 copy-done.4
  217.6 7.6 %shard_map.220 = bf16[8192,128]{1,0:T(8,128)(2,1)} custom-call(s32[4096]{0:T(1024)S(1)} %get-tuple-element.30.row_ref, s32[32]{0:T(128)S(1)} %get-tuple-element.29.count_ref, bf16[4096,128]{1,0:T(8,128)(2,1)S(1)} %bitcast.47, bf16[8192,128]{1,0:T(8,128)(2,1)S(1)} %copy-done.2), custom_call_target="tpu_custom_call" | custom-call | flops 1000000 | bytes 10000000 | tf_op jit(solution)/shard_map/pallas_call | solution.py:275
  (69 shorter events, 0.8 us)
Async XLA Ops:
  9.9 0.6 copy-start.6
  11.0 0.9 copy-start.22
  11.0 1.4 copy-start.24
  11.0 12.2 %copy-start.1 = (bf16[8192,128]{1,0:T(8,128)(2,1)S(1)}, bf16[8192,128]{1,0:T(8,128)(2,1)}, u32[]{:S(2)}) copy-start(bf16[8192,128]{1,0:T(8,128)(2,1)} %table_ref.3) | copy-start | bytes 6291460
  22.5 0.6 copy-start.21
  33.0 1.6 copy-start
  34.6 7.0 %copy-start.27 = (f32[128]{0:T(128)S(1)}, f32[128]{0:T(128)}, u32[]{:S(2)}) copy-start(f32[128]{0:T(128)} %param.27) | copy-start | bytes 1540
  34.6 7.0 %copy-start.28 = (f32[128]{0:T(128)S(1)}, f32[128]{0:T(128)}, u32[]{:S(2)}) copy-start(f32[128]{0:T(128)} %param.26) | copy-start | bytes 1540
  34.6 7.1 %copy-start.25 = (s32[512]{0:T(512)S(1)}, s32[512]{0:T(512)}, u32[]{:S(2)}) copy-start(s32[512]{0:T(512)} %param.23) | copy-start | bytes 6148
  34.6 7.1 %copy-start.26 = (s32[512]{0:T(512)S(1)}, s32[512]{0:T(512)}, u32[]{:S(2)}) copy-start(s32[512]{0:T(512)} %param.24) | copy-start | bytes 6148
  34.6 7.1 %copy-start.23 = (s32[512,10]{0,1:T(8,128)S(1)}, s32[512,10]{0,1:T(8,128)}, u32[]{:S(2)}) copy-start(s32[512,10]{0,1:T(8,128)} %param.25) | copy-start | bytes 61444
  34.7 44.3 %copy-start.10 = (f32[512]{0:T(512)S(1)}, f32[512]{0:T(512)}, u32[]{:S(2)}) copy-start(f32[512]{0:T(512)} %param.30) | copy-start | bytes 6148
  34.7 44.3 %all-to-all-start.1 = ((bf16[8,1536,128]{2,1,0:T(8,128)(2,1)}), bf16[8,1536,128]{2,1,0:T(8,128)(2,1)S(1)}, u32[]{:S(2)}, u32[]{:S(2)}) async-start(bf16[8,1536,128]{2,1,0:T(8,128)(2,1)} %bitcast.46), calls=%async_computation.1 | async-start | bytes 6291456 | tf_op jit(solution)/shard_map/all_to_all | solution.py:319
  42.0 54.9 %copy-start.19 = (f32[128]{0:T(128)S(1)}, f32[128]{0:T(128)}, u32[]{:S(2)}) copy-start(f32[128]{0:T(128)} %param.34) | copy-start | bytes 1540
  79.0 0.7 copy-start.7
  79.7 0.9 copy-start.8
  80.7 0.9 copy-start.9
  91.1 0.7 copy-start.5
  91.8 1.1 copy-start.11
  92.9 0.7 copy-start.15
  93.5 21.8 %all-to-all-start.2 = ((bf16[8,128,128]{2,1,0:T(8,128)(2,1)}), bf16[8,128,128]{2,1,0:T(8,128)(2,1)S(1)}, u32[]{:S(2)}, u32[]{:S(2)}) async-start(bf16[8,128,128]{2,1,0:T(8,128)(2,1)} %bitcast.48), calls=%async_computation.2 | async-start | bytes 524288 | tf_op jit(solution)/shard_map/all_to_all | solution.py:335
  97.0 1.3 copy-start.3
  98.3 1.3 copy-start.12
  99.6 0.9 copy-start.13
  100.5 0.9 copy-start.14
  101.5 0.9 copy-start.16
  102.4 0.8 copy-start.17
  103.2 0.8 copy-start.18
  115.4 101.0 %copy-start.2 = (bf16[8192,128]{1,0:T(8,128)(2,1)S(1)}, bf16[8192,128]{1,0:T(8,128)(2,1)}, u32[]{:S(2)}) copy-start(bf16[8192,128]{1,0:T(8,128)(2,1)} %table_ref.3) | copy-start | bytes 6291460
  115.4 6.8 %copy-start.20 = (bf16[8,128,128]{2,1,0:T(8,128)(2,1)}, bf16[8,128,128]{2,1,0:T(8,128)(2,1)S(1)}, u32[]{:S(2)}) copy-start(bf16[8,128,128]{2,1,0:T(8,128)(2,1)S(1)} %all-to-all-done.2) | copy-start | bytes 786436
  115.4 29.1 %all-to-all-start.3 = ((f32[32,32,128]{2,1,0:T(8,128)}), f32[32,32,128]{2,1,0:T(8,128)S(1)}, u32[]{:S(2)}, u32[]{:S(2)}) async-start(f32[32,32,128]{2,1,0:T(8,128)} %bitcast.20), calls=%async_computation.3 | async-start | bytes 1048576 | tf_op jit(solution)/shard_map/all_to_all | solution.py:345
  122.1 94.3 %all-gather.2.cloned.1.call-start = ((), (), s32[]{:S(2)}) async-start(), calls=%async_computation.4 | async-start | bytes 1310720 | tf_op jit(solution)/shard_map/all_gather | solution.py:336
  216.4 1.2 copy-start.4
Sparse Core Ops, SparseCore 0:
  124.5 31.5 all-gather.1

commit v3 on v2

--- a/solution.py
+++ b/solution.py
@@ -343,7 +343,8 @@
     )
     both = ("node", "batch")
     parts = lax.all_to_all(packed.reshape(devices, -1, LANES), both, split_axis=0, concat_axis=0, tiled=True)
-    total = lax.all_gather(jnp.sum(parts, axis=0), both, axis=0, tiled=True)
+    share = jnp.broadcast_to(jnp.sum(parts, axis=0)[None], parts.shape)
+    total = lax.all_to_all(share, both, split_axis=0, concat_axis=0, tiled=True).reshape(-1, LANES)
     memory_out = write_back(near_row, near_count, fresh, memory, owner_count, batch_count, near_cap)
     kv_end = mem + 2 * (mem + time)
     grad_kv = jnp.concatenate([total[mem : mem + mem + time], total[mem + mem + time : kv_end]], axis=1)

time: 233 us -> 190 us (0.82)
  blocking collectives: 100 us -> 38.4 us
  waiting for transfers between devices: 34.6 us -> 48.3 us
  starting transfers between devices: 16.6 us -> 21.1 us
    all_gather x1 -> x0, blocking collectives: 69.3 us -> none  [on_device(): total = lax.all_gather(jnp.sum(parts, axis=0), both, axis=0, tiled=True)]
    all_to_all x1, waiting for transfers between devices: 0.01 us -> 13.6 us  [on_device(): lax.all_to_all(packed.reshape(devices, -1, LANES), both, split_axis=0, co...]
    all_gather x1, blocking collectives: 20.8 us -> 28.5 us  [on_device(): near_got = lax.all_gather(asked[:, cap:], 'batch', axis=0, tiled=True)]
    all_to_all x0 -> x1, starting transfers between devices: none -> 4.08 us  [on_device(): lax.all_to_all(share, both, split_axis=0, concat_axis=0, tiled=True)]
  transfers between devices with their start and end apart: 4 -> 5, of which waited for: 1 -> 2; matrix products, arithmetic and copies ran while one was open for 3% -> 3% of each run, Pallas kernels for 5% -> 10%
where the time goes in v3:
time: 190 us; the launch traced here: 189 us
  waiting for transfers between devices  48.3 us (25%)
  blocking collectives  38.4 us (20%)
  Pallas kernels  38.4 us (20%)
  starting transfers between devices  21.1 us (11%)
  local copies, waits for them, and re-layouts  20.3 us (11%)
  between operations  14.4 us (8%)
  other arithmetic  6.89 us (4%)
    all_to_all x1, waiting for transfers between devices, on_device(): back = to_all(sent.reshape(owner_count, cap, mem)).reshape(-1, mem)  33.9 us
    all_gather x1, blocking collectives, on_device(): near_got = lax.all_gather(asked[:, cap:], 'batch', axis=0, tiled=True)  28.5 us
    unnamed x60, local copies, waits for them, and re-layouts  16.7 us
    all_to_all x1, waiting for transfers between devices, on_device(): lax.all_to_all(packed.reshape(devices, -1, LANES), both, split_axis=0, co...  13.6 us
    pallas_call x1, Pallas kernels, attend(): pl.pallas_call(functools.partial(attend_kernel, nb), grid=(events // bloc...  11.4 us
    pallas_call x1, Pallas kernels, gather(): pl.pallas_call(functools.partial(gather_kernel, owner_count, cap), out_sh...  9.93 us
    all_to_all x1, blocking collectives, on_device(): asked = to_all(jnp.concatenate([ask, near_ask], axis=1))  9.92 us
    pallas_call x1, Pallas kernels, update(): pl.pallas_call(functools.partial(update_kernel, events, per_event), out_s...  9.56 us
  transfers between devices with their start and end apart: 5, of which 2 were waited for; matrix products, arithmetic and copies ran while one was open for 3% of the time, Pallas kernels for 10%

profile of v3, /device:TPU:0, one launch (start us, length us, event | category | flops | bytes accessed | tf_op | source)
XLA Modules:
  0.0 189.4 jit_solution(5801213920011152695)
XLA Ops:
  7.2 0.7 copy.32
  7.9 0.7 broadcast_multiply_fusion
  8.9 0.2 fusion.7
  9.1 0.8 add_add_fusion
  10.0 0.6 copy-done.6
  10.6 0.4 select_convert_fusion.1
  11.0 0.8 fusion.8
  12.0 0.2 fusion.48
  12.2 0.2 fusion.12
  12.4 0.2 convolution_convert_fusion
  12.6 9.9 %all_to_all.32 = s32[8,1,1664]{2,1,0:T(1,128)S(1)} all-to-all(s32[8,1,1664]{2,1,0:T(1,128)S(1)} %all_to_all.20), channel_id=1, replica_groups=mesh['node'=8,'batch'=4] {'node'}, dimensions={0} | all-to-all | bytes 106496 | tf_op jit(solution)/shard_map/all_to_all | solution.py:314
  22.6 0.5 copy-done.21
  23.1 9.9 %shard_map.217 = bf16[12288,128]{1,0:T(8,128)(2,1)S(1)} custom-call(s32[12288]{0:T(1024)S(1)} %reshape.221.index_ref, s32[8]{0:T(128)S(1)} %get-tuple-element.23.count_ref, bf16[8192,128]{1,0:T(8,128)(2,1)S(1)} %copy-done.1), custom_call_target="tpu_custom_call" | custom-call | flops 1000000 | bytes 10000000 | tf_op jit(solution)/shard_map/pallas_call | solution.py:83
  33.1 1.6 copy-done
  34.8 7.7 %all-to-all-start.1 = ((bf16[8,1536,128]{2,1,0:T(8,128)(2,1)}), bf16[8,1536,128]{2,1,0:T(8,128)(2,1)S(1)}, u32[]{:S(2)}, u32[]{:S(2)}) async-start(bf16[8,1536,128]{2,1,0:T(8,128)(2,1)} %bitcast.51), calls=%async_computation.1 | async-start | bytes 6291456 | tf_op jit(solution)/shard_map/all_to_all | solution.py:319
  42.5 0.4 select_reduce_fusion
  43.1 0.3 add_convert_fusion.1.code_ref
  43.4 3.0 %add_convert_fusion.code_ref = bf16[10,512,128]{2,1,0:T(8,128)(2,1)} fusion(f32[128]{0:T(128)S(1)} %get-tuple-element.41, f32[128]{0:T(128)S(1)} %get-tuple-element.42, f32[10,512]{1,0:T(8,128)S(1)} %convert_bitcast_fusion), kind=kLoop, calls=%fused_computation.4 | loop fusion | flops 14417920 | bytes 1332224 | tf_op jit(solution)/shard_map/convert_element_type | solution.py:27
  46.5 33.9 %all-to-all-done.1 = bf16[8,1536,128]{2,1,0:T(8,128)(2,1)S(1)} async-done(((bf16[8,1536,128]{2,1,0:T(8,128)(2,1)}), bf16[8,1536,128]{2,1,0:T(8,128)(2,1)S(1)}, u32[]{:S(2)}, u32[]{:S(2)}) %all-to-all-start.1) | async-done | bytes 3145760 | tf_op jit(solution)/shard_map/all_to_all | solution.py:319
  80.4 0.7 copy-done.7
  81.1 0.9 copy-done.8
  82.0 0.9 copy-done.9
  82.9 9.6 %shard_map.218 = (bf16[5120,128]{1,0:T(8,128)(2,1)S(1)}, bf16[512,128]{1,0:T(8,128)(2,1)S(1)}, bf16[1024,128]{1,0:T(8,128)(2,1)S(1)}) custom-call(s32[6144]{0:T(1024)S(1)} %copy-done.7, bf16[12288,128]{1,0:T(8,128)(2,1)S(1)} %bitcast.50, bf16[512,128]{1,0:T(8,128)(2,1)S(1)} %add_convert_fusion.1.code_ref, s32[512,1]{1,0:T(8,128)S(1)} %copy.26.pick_ref, ...), custom_call_target="tpu_custom_call" | custom-call | flops 1000000 | bytes 10000000 | tf_op jit(solution)/shard_map/pallas_call | solution.py:135
  92.5 0.7 copy-done.5
  93.2 1.1 copy-done.11
  94.3 0.7 copy-done.15
  94.9 3.4 %all-to-all-start.2 = ((bf16[8,128,128]{2,1,0:T(8,128)(2,1)}), bf16[8,128,128]{2,1,0:T(8,128)(2,1)S(1)}, u32[]{:S(2)}, u32[]{:S(2)}) async-start(bf16[8,128,128]{2,1,0:T(8,128)(2,1)} %bitcast.53), calls=%async_computation.2 | async-start | bytes 524288 | tf_op jit(solution)/shard_map/all_to_all | solution.py:335
  98.4 1.3 copy-done.3
  99.7 1.3 copy-done.12
  101.0 0.9 copy-done.13
  101.9 0.9 copy-done.14
  102.8 0.9 copy-done.16
  103.8 0.8 copy-done.17
  104.6 0.8 copy-done.18
  105.3 11.4 %shard_map.219 = (f32[512,128]{1,0:T(8,128)}, f32[1024,128]{1,0:T(8,128)}) custom-call(bf16[10,512,128]{2,1,0:T(8,128)(2,1)S(1)} %bitcast.55, bf16[10,512,128]{2,1,0:T(8,128)(2,1)S(1)} %copy-done.3, bf16[512,128]{1,0:T(8,128)(2,1)S(1)} %copy-done.16, f32[512,128]{1,0:T(8,128)S(1)} %copy-done.13, bf16[128,128]{1,0:T(8,128)(2,1)S(1)} %copy-done.18, ...), custom_call_target="tpu_custom_call" | custom-call | flops 3000000000 | bytes 10000000 | tf_op jit(solution)/shard_map/pallas_call | solution.py:224
  116.8 5.8 %all-to-all-start.3 = ((f32[32,32,128]{2,1,0:T(8,128)}), f32[32,32,128]{2,1,0:T(8,128)S(1)}, u32[]{:S(2)}, u32[]{:S(2)}) async-start(f32[32,32,128]{2,1,0:T(8,128)} %bitcast.20), calls=%async_computation.3 | async-start | bytes 1048576 | tf_op jit(solution)/shard_map/all_to_all | solution.py:345
  122.6 0.7 all-gather.2.cloned.1.call-update
  123.3 13.6 %all-to-all-done.3 = f32[32,32,128]{2,1,0:T(8,128)S(1)} async-done(((f32[32,32,128]{2,1,0:T(8,128)}), f32[32,32,128]{2,1,0:T(8,128)S(1)}, u32[]{:S(2)}, u32[]{:S(2)}) %all-to-all-start.3) | async-done | bytes 524320 | tf_op jit(solution)/shard_map/all_to_all | solution.py:345
  137.0 0.9 broadcast_in_dim.127
  137.9 4.1 %all-to-all-start.4 = ((f32[32,32,128]{2,1,0:T(8,128)}), f32[32,32,128]{2,1,0:T(8,128)S(1)}, u32[]{:S(2)}, u32[]{:S(2)}) async-start(f32[32,32,128]{2,1,0:T(8,128)} %broadcast_in_dim.127), calls=%async_computation.4 | async-start | bytes 1048576 | tf_op jit(solution)/shard_map/all_to_all | solution.py:347
  141.9 0.7 slice.65
  142.6 28.5 %all_gather.6 = s32[32,128]{1,0:T(8,128)S(1)} all-gather(s32[8,128]{1,0:T(8,128)S(1)} %slice.65), channel_id=1, replica_groups=mesh['node'=8,'batch'=4] {'batch'}, dimensions={0}, use_global_device_ids=true | all-gather | bytes 20480 | tf_op jit(solution)/shard_map/all_gather | solution.py:321
  171.3 1.2 copy-done.4
  172.5 7.5 %shard_map.220 = bf16[8192,128]{1,0:T(8,128)(2,1)} custom-call(s32[4096]{0:T(1024)S(1)} %get-tuple-element.30.row_ref, s32[32]{0:T(128)S(1)} %get-tuple-element.29.count_ref, bf16[4096,128]{1,0:T(8,128)(2,1)S(1)} %bitcast.52, bf16[8192,128]{1,0:T(8,128)(2,1)S(1)} %copy-done.2), custom_call_target="tpu_custom_call" | custom-call | flops 1000000 | bytes 10000000 | tf_op jit(solution)/shard_map/pallas_call | solution.py:275
  180.0 0.5 slice_bitcast_fusion
  180.5 0.7 fusion.62
  181.2 0.7 pad_maximum_fusion
  181.9 0.6 slice.66
  (71 shorter events, 1.1 us)
Async XLA Ops:
  9.9 0.6 copy-start.6
  11.0 0.9 copy-start.22
  11.0 1.4 copy-start.24
  11.0 12.2 %copy-start.1 = (bf16[8192,128]{1,0:T(8,128)(2,1)S(1)}, bf16[8192,128]{1,0:T(8,128)(2,1)}, u32[]{:S(2)}) copy-start(bf16[8192,128]{1,0:T(8,128)(2,1)} %table_ref.3) | copy-start | bytes 6291460
  22.5 0.6 copy-start.21
  33.1 1.6 copy-start
  34.7 8.3 %copy-start.27 = (f32[128]{0:T(128)S(1)}, f32[128]{0:T(128)}, u32[]{:S(2)}) copy-start(f32[128]{0:T(128)} %param.27) | copy-start | bytes 1540
  34.7 8.3 %copy-start.28 = (f32[128]{0:T(128)S(1)}, f32[128]{0:T(128)}, u32[]{:S(2)}) copy-start(f32[128]{0:T(128)} %param.26) | copy-start | bytes 1540
  34.7 8.4 %copy-start.25 = (s32[512]{0:T(512)S(1)}, s32[512]{0:T(512)}, u32[]{:S(2)}) copy-start(s32[512]{0:T(512)} %param.23) | copy-start | bytes 6148
  34.7 8.4 %copy-start.26 = (s32[512]{0:T(512)S(1)}, s32[512]{0:T(512)}, u32[]{:S(2)}) copy-start(s32[512]{0:T(512)} %param.24) | copy-start | bytes 6148
  34.7 8.4 %copy-start.23 = (s32[512,10]{0,1:T(8,128)S(1)}, s32[512,10]{0,1:T(8,128)}, u32[]{:S(2)}) copy-start(s32[512,10]{0,1:T(8,128)} %param.25) | copy-start | bytes 61444
  34.7 45.6 %copy-start.10 = (f32[512]{0:T(512)S(1)}, f32[512]{0:T(512)}, u32[]{:S(2)}) copy-start(f32[512]{0:T(512)} %param.30) | copy-start | bytes 6148
  34.8 45.6 %all-to-all-start.1 = ((bf16[8,1536,128]{2,1,0:T(8,128)(2,1)}), bf16[8,1536,128]{2,1,0:T(8,128)(2,1)S(1)}, u32[]{:S(2)}, u32[]{:S(2)}) async-start(bf16[8,1536,128]{2,1,0:T(8,128)(2,1)} %bitcast.51), calls=%async_computation.1 | async-start | bytes 6291456 | tf_op jit(solution)/shard_map/all_to_all | solution.py:319
  43.4 54.9 %copy-start.19 = (f32[128]{0:T(128)S(1)}, f32[128]{0:T(128)}, u32[]{:S(2)}) copy-start(f32[128]{0:T(128)} %param.34) | copy-start | bytes 1540
  80.4 0.7 copy-start.7
  81.1 0.9 copy-start.8
  82.0 0.9 copy-start.9
  92.5 0.7 copy-start.5
  93.2 1.1 copy-start.11
  94.3 0.7 copy-start.15
  94.9 21.8 %all-to-all-start.2 = ((bf16[8,128,128]{2,1,0:T(8,128)(2,1)}), bf16[8,128,128]{2,1,0:T(8,128)(2,1)S(1)}, u32[]{:S(2)}, u32[]{:S(2)}) async-start(bf16[8,128,128]{2,1,0:T(8,128)(2,1)} %bitcast.53), calls=%async_computation.2 | async-start | bytes 524288 | tf_op jit(solution)/shard_map/all_to_all | solution.py:335
  98.4 1.3 copy-start.3
  99.7 1.3 copy-start.12
  101.0 0.9 copy-start.13
  101.9 0.9 copy-start.14
  102.8 0.9 copy-start.16
  103.8 0.8 copy-start.17
  104.6 0.8 copy-start.18
  116.7 54.5 %copy-start.2 = (bf16[8192,128]{1,0:T(8,128)(2,1)S(1)}, bf16[8192,128]{1,0:T(8,128)(2,1)}, u32[]{:S(2)}) copy-start(bf16[8192,128]{1,0:T(8,128)(2,1)} %table_ref.3) | copy-start | bytes 6291460
  116.8 5.9 %copy-start.20 = (bf16[8,128,128]{2,1,0:T(8,128)(2,1)}, bf16[8,128,128]{2,1,0:T(8,128)(2,1)S(1)}, u32[]{:S(2)}) copy-start(bf16[8,128,128]{2,1,0:T(8,128)(2,1)S(1)} %all-to-all-done.2) | copy-start | bytes 786436
  116.8 20.2 %all-to-all-start.3 = ((f32[32,32,128]{2,1,0:T(8,128)}), f32[32,32,128]{2,1,0:T(8,128)S(1)}, u32[]{:S(2)}, u32[]{:S(2)}) async-start(f32[32,32,128]{2,1,0:T(8,128)} %bitcast.20), calls=%async_computation.3 | async-start | bytes 1048576 | tf_op jit(solution)/shard_map/all_to_all | solution.py:345
  122.6 48.7 %all-gather.2.cloned.1.call-start = ((), (), s32[]{:S(2)}) async-start(), calls=%async_computation.5 | async-start | bytes 1310720 | tf_op jit(solution)/shard_map/all_gather | solution.py:336
  137.9 42.1 %all-to-all-start.4 = ((f32[32,32,128]{2,1,0:T(8,128)}), f32[32,32,128]{2,1,0:T(8,128)S(1)}, u32[]{:S(2)}, u32[]{:S(2)}) async-start(f32[32,32,128]{2,1,0:T(8,128)} %broadcast_in_dim.127), calls=%async_computation.4 | async-start | bytes 1048576 | tf_op jit(solution)/shard_map/all_to_all | solution.py:347
  171.3 1.2 copy-start.4
Sparse Core Ops, SparseCore 0:
  125.5 39.9 all-gather.1
